TPU v7x, 128 devices: a whole 4x4x4 slice. The times are simulated.
128 devices in a mesh: gx: 16 (over y, z_lo, core), gy: 8 (over x, z_hi).
Axes of the slice: x: 4, y: 4, z: 4 (z_hi: 2, z_lo: 2; z = z_hi * 2 + z_lo), core: 2. Of those that a mesh axis runs over, the one named last changes fastest.
Arguments:
- thermal_anomaly_grid: float32 [30, 256, 2048], P(None, 'gy', 'gx'), may hold values from -5 to 5
- relative_moisture: float32 [30, 256, 2048], P(None, 'gy', 'gx'), may hold values from 0.05 to 1
- overcast_share: float32 [30, 256, 2048], P(None, 'gy', 'gx'), may hold values from 0 to 1
- sun_angle_projection: float32 [256, 2048], P('gy', 'gx'), may hold values from 0.1 to 1
- daylight_mask: int32 [16, 256], P('gx', 'gy'), may hold values 0 or 1
- radiator_owner_position: int32 [16, 256, 1], P('gx', 'gy'), may hold values from 0 to 15; in each aligned block of 32 rows (0 to 31, 32 to 63, ..., all dimensions but the last counted through in order) at most 4 rows name the same one
- molecular_opacity_lookup: bfloat16 [30, 140, 128], replicated, may hold values from 0.019897461 to 1.5
- condensed_opacity_per_share: float32 [140], replicated, may hold values from 0.05 to 1
- planck_emission_factor: float32 [140], replicated, may hold values from 0.2 to 1
- insolation_quadrature_factor: float32 [140], replicated, may hold values from 0.2 to 2
Outputs:
- advanced_anomaly_grid: float32 [30, 256, 2048], P(None, 'gy', 'gx')
- humidity_next: float32 [30, 256, 2048], P(None, 'gy', 'gx')
- ground_irradiance_slots: float32 [8, 16, 16, 4, 128], P('gy', 'gx')
Inputs may be any that keep to these rules, and one draw needn't show every extreme that they name: `radiator_owner_position`: among the 32 blocks of one device, at most 4 name the same host, and some device's blocks name one host exactly 4 times.
All inputs are finite; a program needn't handle non-finite values. No bound on the sum of `daylight_mask` on one device may be relied on, other than what follows from the above.
Results may differ from a plain program's by a relative error of at most 0.0034.
Values may be sent and summed in bfloat16 or wider, within the bound.
A program may use at most 128 MiB of HBM per device.

v0:
```python
import jax
import jax.numpy as jnp
from jax import lax
from jax.sharding import PartitionSpec as P

NT = 16
NQ = 8


diffusion = 0.2
diffusivity = 1.66


def extended(block, sides, width):
    for axis, dim in sides:
        count = lax.axis_size(axis)
        forward = [(i, i + 1) for i in range(count - 1)]
        backward = [(target, source) for source, target in forward]
        low = lax.ppermute(
            lax.slice_in_dim(block, block.shape[dim] - width, None, axis=dim), axis, forward
        )
        high = lax.ppermute(lax.slice_in_dim(block, 0, width, axis=dim), axis, backward)
        block = jnp.concatenate([low, block, high], axis=dim)
    return block


def stencil(bordered_grid):
    centre = bordered_grid[:, :, 1:-1, 1:-1]
    beside_all = (
        bordered_grid[:, :, 2:, 1:-1]
        + bordered_grid[:, :, :-2, 1:-1]
        + bordered_grid[:, :, 1:-1, 2:]
        + bordered_grid[:, :, 1:-1, :-2]
    )
    return centre + diffusion * (beside_all - 4.0 * centre)


def optical_depth(layer, table_layer, condensed_opacity_per_share):
    air_temp, moisture, condensate = (layer[0], layer[1], layer[2])
    temp_nodes = jnp.arange(NT, dtype=jnp.float32)
    humid_nodes = jnp.arange(NQ, dtype=jnp.float32)
    temp_pos = jnp.clip((air_temp + 3.0) * ((NT - 1.0) / 6.0), 0.0, NT - 1.0)
    humid_pos = jnp.clip(moisture * (NQ - 1.0), 0.0, NQ - 1.0)
    temp_hat = jnp.maximum(0.0, 1.0 - jnp.abs(temp_pos[None, :] - temp_nodes[:, None]))
    humid_hat = jnp.maximum(0.0, 1.0 - jnp.abs(humid_pos[None, :] - humid_nodes[:, None]))
    weights = (
        (temp_hat[:, None, :] * humid_hat[None, :, :]).reshape(NT * NQ, -1).astype(jnp.bfloat16)
    )
    gas_depth = jnp.dot(table_layer, weights, preferred_element_type=jnp.float32)
    return gas_depth + condensed_opacity_per_share[:, None] * condensate[None, :]


def column_physics(
    prognostic_bundle,
    zenith,
    incident,
    molecular_opacity_lookup,
    condensed_opacity_per_share,
    planck_emission_factor,
    insolation_quadrature_factor,
):
    layers = jnp.transpose(prognostic_bundle, (1, 0, 2))
    gpoints = planck_emission_factor.shape[0]

    def downward(carry, inputs):
        long_down, short_down = carry
        layer, table_layer = inputs
        depth = optical_depth(layer, table_layer, condensed_opacity_per_share)
        through = jnp.exp(-diffusivity * depth)
        source = planck_emission_factor[:, None] * (1.0 + 0.25 * layer[0][None, :])
        long_next = long_down * through + (1.0 - through) * source
        short_next = short_down * jnp.exp(-depth / zenith[None, :])
        gained = jnp.sum(long_down - long_next + short_down - short_next, axis=0)
        return ((long_next, short_next), gained)

    def upward(long_up, inputs):
        layer, table_layer = inputs
        depth = optical_depth(layer, table_layer, condensed_opacity_per_share)
        through = jnp.exp(-diffusivity * depth)
        source = planck_emission_factor[:, None] * (1.0 + 0.25 * layer[0][None, :])
        long_next = long_up * through + (1.0 - through) * source
        return (long_next, jnp.sum(long_up - long_next, axis=0))

    start_long = jnp.zeros((gpoints, prognostic_bundle.shape[2]), jnp.float32)
    start_short = insolation_quadrature_factor[:, None] * incident[None, :]
    bottom, down_gain = lax.scan(
        downward, (start_long, start_short), (layers, molecular_opacity_lookup)
    )
    start_up = planck_emission_factor[:, None] * (1.0 + 0.25 * layers[-1, 0][None, :])
    top_up, up_gain = lax.scan(upward, start_up, (layers, molecular_opacity_lookup), reverse=True)
    heating = 2.0 / gpoints * (down_gain + up_gain)
    ground_irradiance_result = jnp.sum(bottom[0] + bottom[1], axis=0) / gpoints
    return (heating, ground_irradiance_result)


def block_rank(hosts):
    profile_groups = hosts.shape[-1]
    earlier = jnp.arange(profile_groups)[None, :] < jnp.arange(profile_groups)[:, None]
    same = hosts[..., :, None] == hosts[..., None, :]
    return jnp.sum(jnp.logical_and(same, earlier), axis=-1)


def slot_table(hosts, host_ids, capacity):
    rank = block_rank(hosts)
    slot_ids = jnp.arange(capacity, dtype=jnp.int32)[None, :, None]
    chosen = jnp.logical_and(
        hosts[..., None, None, :] == host_ids[:, None, None], rank[..., None, None, :] == slot_ids
    )
    return chosen.astype(jnp.float32)


def radiate(
    received_state,
    received_light,
    molecular_opacity_lookup,
    condensed_opacity_per_share,
    planck_emission_factor,
    insolation_quadrature_factor,
):
    sources, items = (received_state.shape[0], received_state.shape[1])
    level_count, width = (received_state.shape[3], received_state.shape[4])
    columns = sources * items * width
    prognostic_bundle = (
        jnp.transpose(received_state, (2, 3, 0, 1, 4))
        .reshape(3, level_count, columns)
        .astype(jnp.float32)
    )
    shine = jnp.transpose(received_light, (2, 0, 1, 3)).reshape(2, columns).astype(jnp.float32)
    occupied = shine[0] > 0.0
    zenith = jnp.where(occupied, shine[0], 1.0)
    heating, ground_irradiance_result = column_physics(
        prognostic_bundle,
        zenith,
        shine[1],
        molecular_opacity_lookup,
        condensed_opacity_per_share,
        planck_emission_factor,
        insolation_quadrature_factor,
    )
    ground_irradiance_result = jnp.where(occupied, ground_irradiance_result, 0.0)
    heating = jnp.transpose(heating.reshape(level_count, sources, items, width), (1, 2, 0, 3))
    return (heating, ground_irradiance_result.reshape(sources, items, width))


def on_device(
    thermal_anomaly_grid,
    relative_moisture,
    overcast_share,
    sun_angle_projection,
    daylight_mask,
    radiator_owner_position,
    molecular_opacity_lookup,
    condensed_opacity_per_share,
    planck_emission_factor,
    insolation_quadrature_factor,
):
    host_count = lax.axis_size("gx")
    profile_groups = thermal_anomaly_grid.shape[1]
    capacity = max(2, (2 * profile_groups + host_count - 1) // host_count)
    bordered_grid = extended(
        jnp.stack((thermal_anomaly_grid, relative_moisture)), (("gx", 3), ("gy", 2)), 1
    )
    laplacian_blurred_grid = stencil(bordered_grid)
    prognostic_bundle = jnp.stack((thermal_anomaly_grid, relative_moisture, overcast_share)).astype(
        jnp.bfloat16
    )
    lit_rows = daylight_mask[0].astype(jnp.float32)[:, None]
    light = jnp.stack((sun_angle_projection, sun_angle_projection * lit_rows)).astype(jnp.bfloat16)
    own_hosts = radiator_owner_position[0, :, 0]
    slot_position = own_hosts * capacity + block_rank(own_hosts)
    every_state, every_light, every_host = (
        lax.all_gather(prognostic_bundle[None], "gx", axis=0, tiled=True),
        lax.all_gather(light[None], "gx", axis=0, tiled=True),
        lax.all_gather(own_hosts[None], "gx", axis=0, tiled=True),
    )
    mine = jnp.reshape(lax.axis_index("gx"), (1,))
    chooser = slot_table(every_host, mine, capacity)[:, 0].astype(jnp.bfloat16)
    received_state = jnp.einsum(
        "skb,sclbx->skclx", chooser, every_state, preferred_element_type=jnp.float32
    ).astype(jnp.bfloat16)
    received_light = jnp.einsum(
        "skb,scbx->skcx", chooser, every_light, preferred_element_type=jnp.float32
    ).astype(jnp.bfloat16)
    heating, ground_irradiance_result = radiate(
        received_state,
        received_light,
        molecular_opacity_lookup,
        condensed_opacity_per_share,
        planck_emission_factor,
        insolation_quadrature_factor,
    )
    returned = lax.all_to_all(heating, "gx", split_axis=0, concat_axis=0, tiled=True)
    flat_returned = returned.reshape(
        returned.shape[0] * returned.shape[1], returned.shape[2], returned.shape[3]
    )
    own_warming_rates = jnp.transpose(flat_returned[slot_position], (1, 0, 2))
    advanced_anomaly_grid = laplacian_blurred_grid[0] + own_warming_rates
    return (advanced_anomaly_grid, laplacian_blurred_grid[1], ground_irradiance_result[None, None])


def solution(mesh):
    placed = (
        P(None, "gy", "gx"),
        P(None, "gy", "gx"),
        P(None, "gy", "gx"),
        P("gy", "gx"),
        P("gx", "gy"),
        P("gx", "gy", None),
        P(),
        P(),
        P(),
        P(),
    )
    return jax.shard_map(
        on_device,
        mesh=mesh,
        in_specs=placed,
        out_specs=(P(None, "gy", "gx"), P(None, "gy", "gx"), P("gy", "gx", None, None, None)),
        check_vma=False,
    )
```

profile of v0, /device:TPU:1, one launch (start us, length us, event | category | flops | bytes accessed | tf_op | source)
XLA Modules:
  0.0 643.7 jit_solution(1116959172714404542)
XLA Ops:
  19.9 20.2 %all-gather = s32[16,32,1]{1,2,0:T(1,128)S(1)} all-gather(s32[1,32,1]{1,2,0:T(1,128)S(1)} %copy-done.6), channel_id=2, replica_groups=mesh['gx'=16,'gy'=8] {'gx'}, dimensions={0}, use_global_device_ids=true | all-gather | bytes 2176 | tf_op jit(solution)/shard_map/all_gather | solution.py:174
  40.8 17.3 %all_gather.10 = bf16[16,2,32,128]{3,2,1,0:T(8,128)(2,1)S(1)} all-gather(bf16[1,2,32,128]{3,2,1,0:T(8,128)(2,1)S(1)} %pad_maximum_fusion.18), channel_id=1, replica_groups=mesh['gx'=16,'gy'=8] {'gx'}, dimensions={0}, use_global_device_ids=true | all-gather | bytes 278528 | tf_op jit(solution)/shard_map/all_gather | solution.py:173
  76.5 11.5 %all-gather.3.cloned.1.call-done = bf16[16,3,30,32,128]{4,3,2,1,0:T(8,128)(2,1)} async-done(((bf16[1,3,30,32,128]{4,3,2,1,0:T(8,128)(2,1)}), bf16[16,3,30,32,128]{4,3,2,1,0:T(8,128)(2,1)}) %all-gather.3.cloned.1.call-update) | async-done | bytes 11796496 | tf_op jit(solution)/shard_map/all_gather | solution.py:172
  106.1 214.3 %while.31 = (s32[]{:T(128)}, f32[140,8192]{1,0:T(8,128)}, f32[30,8192]{1,0:T(8,128)S(1)}, bf16[30,140,128]{2,1,0:T(8,128)(2,1)}, f32[30,3,8192]{2,1,0:T(4,128)},...) while((s32[]{:T(128)}, f32[140,8192]{1,0:T(8,128)}, ...), condition=%wide.region_6.7_spmd, body=%wide.region_4.6_spmd.sunk | while | flops 308002816 | bytes 11375885 | solution.py:90
  320.5 293.4 %while.32 = (s32[]{:T(128)}, f32[140,8192]{1,0:T(8,128)}, f32[140,8192]{1,0:T(8,128)}, f32[30,8192]{1,0:T(8,128)S(1)}, bf16[30,140,128]{2,1,0:T(8,128)(2,1)}, /*...) while((s32[]{:T(128)}, f32[140,8192]{1,0:T(8,128)}, ...), condition=%wide.region_3.4_spmd.clone, body=%wide.region_1.3_spmd.clone.sunk | while | flops 314884096 | bytes 20714776 | solution.py:86
  331.0 8.3 %subtract_reduce_fusion.5 = (f32[8192]{0:T(1024)S(1)}, f32[140,8192]{1,0:T(8,128)}, f32[140,8192]{1,0:T(8,128)}) fusion(f32[140,8192]{1,0:T(8,128)} %get-tuple-element.499, f32[140,8192]{1,0:T(8,128)} %get-tuple-element.498, pred[]{:T(512)S(6)} %compare.3, f32[8192]{0:T(1024)S(1)} %get-tuple-element.518, f32[8192]{0:T(1024)S(1)} %bitcast.125, ...), kind=kOutput, calls=%fused_computation.21.clone.1 | convolution fusion | flops 314040320 | bytes 19567716 | tf_op jit(solution)/shard_map/while/body/eval_jaxpr/dot_general | solution.py:49
  340.8 8.3 %subtract_reduce_fusion.5 = (f32[8192]{0:T(1024)S(1)}, f32[140,8192]{1,0:T(8,128)}, f32[140,8192]{1,0:T(8,128)}) fusion(f32[140,8192]{1,0:T(8,128)} %get-tuple-element.499, f32[140,8192]{1,0:T(8,128)} %get-tuple-element.498, pred[]{:T(512)S(6)} %compare.3, f32[8192]{0:T(1024)S(1)} %get-tuple-element.518, f32[8192]{0:T(1024)S(1)} %bitcast.125, ...), kind=kOutput, calls=%fused_computation.21.clone.1 | convolution fusion | flops 314040320 | bytes 19567716 | tf_op jit(solution)/shard_map/while/body/eval_jaxpr/dot_general | solution.py:49
  350.6 8.3 %subtract_reduce_fusion.5 = (f32[8192]{0:T(1024)S(1)}, f32[140,8192]{1,0:T(8,128)}, f32[140,8192]{1,0:T(8,128)}) fusion(f32[140,8192]{1,0:T(8,128)} %get-tuple-element.499, f32[140,8192]{1,0:T(8,128)} %get-tuple-element.498, pred[]{:T(512)S(6)} %compare.3, f32[8192]{0:T(1024)S(1)} %get-tuple-element.518, f32[8192]{0:T(1024)S(1)} %bitcast.125, ...), kind=kOutput, calls=%fused_computation.21.clone.1 | convolution fusion | flops 314040320 | bytes 19567716 | tf_op jit(solution)/shard_map/while/body/eval_jaxpr/dot_general | solution.py:49
  360.4 8.3 %subtract_reduce_fusion.5 = (f32[8192]{0:T(1024)S(1)}, f32[140,8192]{1,0:T(8,128)}, f32[140,8192]{1,0:T(8,128)}) fusion(f32[140,8192]{1,0:T(8,128)} %get-tuple-element.499, f32[140,8192]{1,0:T(8,128)} %get-tuple-element.498, pred[]{:T(512)S(6)} %compare.3, f32[8192]{0:T(1024)S(1)} %get-tuple-element.518, f32[8192]{0:T(1024)S(1)} %bitcast.125, ...), kind=kOutput, calls=%fused_computation.21.clone.1 | convolution fusion | flops 314040320 | bytes 19567716 | tf_op jit(solution)/shard_map/while/body/eval_jaxpr/dot_general | solution.py:49
  370.2 8.3 %subtract_reduce_fusion.5 = (f32[8192]{0:T(1024)S(1)}, f32[140,8192]{1,0:T(8,128)}, f32[140,8192]{1,0:T(8,128)}) fusion(f32[140,8192]{1,0:T(8,128)} %get-tuple-element.499, f32[140,8192]{1,0:T(8,128)} %get-tuple-element.498, pred[]{:T(512)S(6)} %compare.3, f32[8192]{0:T(1024)S(1)} %get-tuple-element.518, f32[8192]{0:T(1024)S(1)} %bitcast.125, ...), kind=kOutput, calls=%fused_computation.21.clone.1 | convolution fusion | flops 314040320 | bytes 19567716 | tf_op jit(solution)/shard_map/while/body/eval_jaxpr/dot_general | solution.py:49
  399.6 8.3 %subtract_reduce_fusion.5 = (f32[8192]{0:T(1024)S(1)}, f32[140,8192]{1,0:T(8,128)}, f32[140,8192]{1,0:T(8,128)}) fusion(f32[140,8192]{1,0:T(8,128)} %get-tuple-element.499, f32[140,8192]{1,0:T(8,128)} %get-tuple-element.498, pred[]{:T(512)S(6)} %compare.3, f32[8192]{0:T(1024)S(1)} %get-tuple-element.518, f32[8192]{0:T(1024)S(1)} %bitcast.125, ...), kind=kOutput, calls=%fused_computation.21.clone.1 | convolution fusion | flops 314040320 | bytes 19567716 | tf_op jit(solution)/shard_map/while/body/eval_jaxpr/dot_general | solution.py:49
  409.4 8.3 %subtract_reduce_fusion.5 = (f32[8192]{0:T(1024)S(1)}, f32[140,8192]{1,0:T(8,128)}, f32[140,8192]{1,0:T(8,128)}) fusion(f32[140,8192]{1,0:T(8,128)} %get-tuple-element.499, f32[140,8192]{1,0:T(8,128)} %get-tuple-element.498, pred[]{:T(512)S(6)} %compare.3, f32[8192]{0:T(1024)S(1)} %get-tuple-element.518, f32[8192]{0:T(1024)S(1)} %bitcast.125, ...), kind=kOutput, calls=%fused_computation.21.clone.1 | convolution fusion | flops 314040320 | bytes 19567716 | tf_op jit(solution)/shard_map/while/body/eval_jaxpr/dot_general | solution.py:49
  419.2 8.3 %subtract_reduce_fusion.5 = (f32[8192]{0:T(1024)S(1)}, f32[140,8192]{1,0:T(8,128)}, f32[140,8192]{1,0:T(8,128)}) fusion(f32[140,8192]{1,0:T(8,128)} %get-tuple-element.499, f32[140,8192]{1,0:T(8,128)} %get-tuple-element.498, pred[]{:T(512)S(6)} %compare.3, f32[8192]{0:T(1024)S(1)} %get-tuple-element.518, f32[8192]{0:T(1024)S(1)} %bitcast.125, ...), kind=kOutput, calls=%fused_computation.21.clone.1 | convolution fusion | flops 314040320 | bytes 19567716 | tf_op jit(solution)/shard_map/while/body/eval_jaxpr/dot_general | solution.py:49
  458.4 8.3 %subtract_reduce_fusion.5 = (f32[8192]{0:T(1024)S(1)}, f32[140,8192]{1,0:T(8,128)}, f32[140,8192]{1,0:T(8,128)}) fusion(f32[140,8192]{1,0:T(8,128)} %get-tuple-element.499, f32[140,8192]{1,0:T(8,128)} %get-tuple-element.498, pred[]{:T(512)S(6)} %compare.3, f32[8192]{0:T(1024)S(1)} %get-tuple-element.518, f32[8192]{0:T(1024)S(1)} %bitcast.125, ...), kind=kOutput, calls=%fused_computation.21.clone.1 | convolution fusion | flops 314040320 | bytes 19567716 | tf_op jit(solution)/shard_map/while/body/eval_jaxpr/dot_general | solution.py:49
  468.2 8.3 %subtract_reduce_fusion.5 = (f32[8192]{0:T(1024)S(1)}, f32[140,8192]{1,0:T(8,128)}, f32[140,8192]{1,0:T(8,128)}) fusion(f32[140,8192]{1,0:T(8,128)} %get-tuple-element.499, f32[140,8192]{1,0:T(8,128)} %get-tuple-element.498, pred[]{:T(512)S(6)} %compare.3, f32[8192]{0:T(1024)S(1)} %get-tuple-element.518, f32[8192]{0:T(1024)S(1)} %bitcast.125, ...), kind=kOutput, calls=%fused_computation.21.clone.1 | convolution fusion | flops 314040320 | bytes 19567716 | tf_op jit(solution)/shard_map/while/body/eval_jaxpr/dot_general | solution.py:49
  478.0 8.3 %subtract_reduce_fusion.5 = (f32[8192]{0:T(1024)S(1)}, f32[140,8192]{1,0:T(8,128)}, f32[140,8192]{1,0:T(8,128)}) fusion(f32[140,8192]{1,0:T(8,128)} %get-tuple-element.499, f32[140,8192]{1,0:T(8,128)} %get-tuple-element.498, pred[]{:T(512)S(6)} %compare.3, f32[8192]{0:T(1024)S(1)} %get-tuple-element.518, f32[8192]{0:T(1024)S(1)} %bitcast.125, ...), kind=kOutput, calls=%fused_computation.21.clone.1 | convolution fusion | flops 314040320 | bytes 19567716 | tf_op jit(solution)/shard_map/while/body/eval_jaxpr/dot_general | solution.py:49
  487.8 8.3 %subtract_reduce_fusion.5 = (f32[8192]{0:T(1024)S(1)}, f32[140,8192]{1,0:T(8,128)}, f32[140,8192]{1,0:T(8,128)}) fusion(f32[140,8192]{1,0:T(8,128)} %get-tuple-element.499, f32[140,8192]{1,0:T(8,128)} %get-tuple-element.498, pred[]{:T(512)S(6)} %compare.3, f32[8192]{0:T(1024)S(1)} %get-tuple-element.518, f32[8192]{0:T(1024)S(1)} %bitcast.125, ...), kind=kOutput, calls=%fused_computation.21.clone.1 | convolution fusion | flops 314040320 | bytes 19567716 | tf_op jit(solution)/shard_map/while/body/eval_jaxpr/dot_general | solution.py:49
  517.2 8.3 %subtract_reduce_fusion.5 = (f32[8192]{0:T(1024)S(1)}, f32[140,8192]{1,0:T(8,128)}, f32[140,8192]{1,0:T(8,128)}) fusion(f32[140,8192]{1,0:T(8,128)} %get-tuple-element.499, f32[140,8192]{1,0:T(8,128)} %get-tuple-element.498, pred[]{:T(512)S(6)} %compare.3, f32[8192]{0:T(1024)S(1)} %get-tuple-element.518, f32[8192]{0:T(1024)S(1)} %bitcast.125, ...), kind=kOutput, calls=%fused_computation.21.clone.1 | convolution fusion | flops 314040320 | bytes 19567716 | tf_op jit(solution)/shard_map/while/body/eval_jaxpr/dot_general | solution.py:49
  527.0 8.3 %subtract_reduce_fusion.5 = (f32[8192]{0:T(1024)S(1)}, f32[140,8192]{1,0:T(8,128)}, f32[140,8192]{1,0:T(8,128)}) fusion(f32[140,8192]{1,0:T(8,128)} %get-tuple-element.499, f32[140,8192]{1,0:T(8,128)} %get-tuple-element.498, pred[]{:T(512)S(6)} %compare.3, f32[8192]{0:T(1024)S(1)} %get-tuple-element.518, f32[8192]{0:T(1024)S(1)} %bitcast.125, ...), kind=kOutput, calls=%fused_computation.21.clone.1 | convolution fusion | flops 314040320 | bytes 19567716 | tf_op jit(solution)/shard_map/while/body/eval_jaxpr/dot_general | solution.py:49
  536.8 8.3 %subtract_reduce_fusion.5 = (f32[8192]{0:T(1024)S(1)}, f32[140,8192]{1,0:T(8,128)}, f32[140,8192]{1,0:T(8,128)}) fusion(f32[140,8192]{1,0:T(8,128)} %get-tuple-element.499, f32[140,8192]{1,0:T(8,128)} %get-tuple-element.498, pred[]{:T(512)S(6)} %compare.3, f32[8192]{0:T(1024)S(1)} %get-tuple-element.518, f32[8192]{0:T(1024)S(1)} %bitcast.125, ...), kind=kOutput, calls=%fused_computation.21.clone.1 | convolution fusion | flops 314040320 | bytes 19567716 | tf_op jit(solution)/shard_map/while/body/eval_jaxpr/dot_general | solution.py:49
  546.6 8.3 %subtract_reduce_fusion.5 = (f32[8192]{0:T(1024)S(1)}, f32[140,8192]{1,0:T(8,128)}, f32[140,8192]{1,0:T(8,128)}) fusion(f32[140,8192]{1,0:T(8,128)} %get-tuple-element.499, f32[140,8192]{1,0:T(8,128)} %get-tuple-element.498, pred[]{:T(512)S(6)} %compare.3, f32[8192]{0:T(1024)S(1)} %get-tuple-element.518, f32[8192]{0:T(1024)S(1)} %bitcast.125, ...), kind=kOutput, calls=%fused_computation.21.clone.1 | convolution fusion | flops 314040320 | bytes 19567716 | tf_op jit(solution)/shard_map/while/body/eval_jaxpr/dot_general | solution.py:49
  556.4 8.3 %subtract_reduce_fusion.5 = (f32[8192]{0:T(1024)S(1)}, f32[140,8192]{1,0:T(8,128)}, f32[140,8192]{1,0:T(8,128)}) fusion(f32[140,8192]{1,0:T(8,128)} %get-tuple-element.499, f32[140,8192]{1,0:T(8,128)} %get-tuple-element.498, pred[]{:T(512)S(6)} %compare.3, f32[8192]{0:T(1024)S(1)} %get-tuple-element.518, f32[8192]{0:T(1024)S(1)} %bitcast.125, ...), kind=kOutput, calls=%fused_computation.21.clone.1 | convolution fusion | flops 314040320 | bytes 19567716 | tf_op jit(solution)/shard_map/while/body/eval_jaxpr/dot_general | solution.py:49
  566.2 8.3 %subtract_reduce_fusion.5 = (f32[8192]{0:T(1024)S(1)}, f32[140,8192]{1,0:T(8,128)}, f32[140,8192]{1,0:T(8,128)}) fusion(f32[140,8192]{1,0:T(8,128)} %get-tuple-element.499, f32[140,8192]{1,0:T(8,128)} %get-tuple-element.498, pred[]{:T(512)S(6)} %compare.3, f32[8192]{0:T(1024)S(1)} %get-tuple-element.518, f32[8192]{0:T(1024)S(1)} %bitcast.125, ...), kind=kOutput, calls=%fused_computation.21.clone.1 | convolution fusion | flops 314040320 | bytes 19567716 | tf_op jit(solution)/shard_map/while/body/eval_jaxpr/dot_general | solution.py:49
  605.4 8.3 %subtract_reduce_fusion.5 = (f32[8192]{0:T(1024)S(1)}, f32[140,8192]{1,0:T(8,128)}, f32[140,8192]{1,0:T(8,128)}) fusion(f32[140,8192]{1,0:T(8,128)} %get-tuple-element.499, f32[140,8192]{1,0:T(8,128)} %get-tuple-element.498, pred[]{:T(512)S(6)} %compare.3, f32[8192]{0:T(1024)S(1)} %get-tuple-element.518, f32[8192]{0:T(1024)S(1)} %bitcast.125, ...), kind=kOutput, calls=%fused_computation.21.clone.1 | convolution fusion | flops 314040320 | bytes 19567716 | tf_op jit(solution)/shard_map/while/body/eval_jaxpr/dot_general | solution.py:49
  (356 shorter events, 420.6 us)
Async XLA Ops:
  7.2 3.5 copy-start.1
  7.2 3.5 copy-start.2
  7.2 80.8 %all-gather.3.cloned.1.call-start = ((), (), s32[]{:S(2)}) async-start(), calls=%async_computation.1 | async-start | bytes 12533760 | tf_op jit(solution)/shard_map/all_gather | solution.py:172
  9.6 10.2 %copy-start.6 = (s32[1,32,1]{1,2,0:T(1,128)S(1)}, s32[1,32,1]{1,2,0:T(1,128)}, u32[]{:S(2)}) copy-start(s32[1,32,1]{1,2,0:T(1,128)} %param.19) | copy-start | bytes 388
  9.7 30.4 %copy-start.8 = (s32[1,32]{1,0:T(1,128)S(1)}, s32[1,32]{1,0:T(1,128)}, u32[]{:S(2)}) copy-start(s32[1,32]{1,0:T(1,128)} %param.18) | copy-start | bytes 388
  9.7 30.4 %copy-start.3 = (f32[32,128]{1,0:T(8,128)S(1)}, f32[32,128]{1,0:T(8,128)}, u32[]{:S(2)}) copy-start(f32[32,128]{1,0:T(8,128)} %param.17) | copy-start | bytes 49156
  10.6 47.7 %copy-start.4 = (f32[140]{0:T(256)S(1)}, f32[140]{0:T(256)}, u32[]{:S(2)}) copy-start(f32[140]{0:T(256)} %param.23) | copy-start | bytes 1684
  12.3 49.7 %collective-permute-start = (f32[2,30,32,1]{2,0,3,1:T(2,128)S(1)}, f32[2,30,32,1]{2,0,3,1:T(2,128)S(1)}, u32[]{:S(2)}, u32[]{:S(2)}) collective-permute-start(f32[2,30,32,1]{2,0,3,1:T(2,128)S(1)} %copy.52), channel_id=1, source_target_pairs={{0,8},{8,16},{16,24},{24,32},{32,40},{40,48},{48,56},{56,64},{64,7... | collective-permute-start | bytes 23048 | tf_op jit(solution)/shard_map/ppermute | solution.py:19
  18.0 43.1 %collective-permute-start.1 = (f32[2,30,32,1]{2,0,3,1:T(2,128)S(1)}, f32[2,30,32,1]{2,0,3,1:T(2,128)S(1)}, u32[]{:S(2)}, u32[]{:S(2)}) collective-permute-start(f32[2,30,32,1]{2,0,3,1:T(2,128)S(1)} %copy.53), channel_id=1, source_target_pairs={{8,0},{16,8},{24,16},{32,24},{40,32},{48,40},{56,48},{64,56},{72,6... | collective-permute-start | bytes 23048 | tf_op jit(solution)/shard_map/ppermute | solution.py:22
  63.2 9.1 %collective-permute-start.2 = (f32[2,30,1,130]{3,1,2,0:T(8,128)S(1)}, f32[2,30,1,130]{3,1,2,0:T(8,128)S(1)}, u32[]{:S(2)}, u32[]{:S(2)}) collective-permute-start(f32[2,30,1,130]{3,1,2,0:T(8,128)S(1)} %get-tuple-element.348), channel_id=1, source_target_pairs={{1,0},{2,1},{3,2},{4,3},{5,4},{6,5},{7,6},{9,8},{10,9},{11,10},{12... | collective-permute-start | bytes 93608 | tf_op jit(solution)/shard_map/ppermute | solution.py:22
  64.5 9.5 %collective-permute-start.3 = (f32[2,30,1,130]{3,1,2,0:T(8,128)S(1)}, f32[2,30,1,130]{3,1,2,0:T(8,128)S(1)}, u32[]{:S(2)}, u32[]{:S(2)}) collective-permute-start(f32[2,30,1,130]{3,1,2,0:T(8,128)S(1)} %get-tuple-element.349), channel_id=1, source_target_pairs={{0,1},{1,2},{2,3},{3,4},{4,5},{5,6},{6,7},{8,9},{9,10},{10,11},{11... | collective-permute-start | bytes 93608 | tf_op jit(solution)/shard_map/ppermute | solution.py:19
  99.3 4.0 copy-start.5
  99.4 6.7 %copy-start.7 = (f32[140]{0:T(256)S(1)}, f32[140]{0:T(256)}, u32[]{:S(2)}) copy-start(f32[140]{0:T(256)} %param.21) | copy-start | bytes 1684
  615.8 19.2 %all-to-all-start = ((f32[16,4,30,128]{3,1,2,0:T(4,128)}), f32[16,4,30,128]{3,1,2,0:T(4,128)S(1)}, u32[]{:S(2)}, u32[]{:S(2)}) async-start(f32[16,4,30,128]{3,1,2,0:T(4,128)} %copy.61), calls=%async_computation | async-start | bytes 1966080 | tf_op jit(solution)/shard_map/all_to_all | solution.py:192
  622.1 13.6 %copy-start = (f32[2,30,32,128]{3,1,2,0:T(8,128)S(1)}, f32[2,30,32,128]{3,1,2,0:T(8,128)}, u32[]{:S(2)}) copy-start(f32[2,30,32,128]{3,1,2,0:T(8,128)} %fusion.25) | copy-start | bytes 2949124
Sparse Core Ops, SparseCore 0:
  10.8 77.1 all-gather.2
where the time goes:
time: 645 us; the launch traced here: 644 us
  matrix products  423 us (66%)
  other arithmetic  97.6 us (15%)
  blocking collectives  37.5 us (6%)
  local copies, waits for them, and re-layouts  27.6 us (4%)
  waiting for transfers between devices  23 us (4%)
  starting transfers between devices  18.2 us (3%)
  between operations  14.4 us (2%)
    dot_general x60, matrix products, optical_depth(): jnp.dot(table_layer, weights, preferred_element_type=jnp.float32)  417 us
    min x30, other arithmetic, optical_depth(): temp_pos = jnp.clip((air_temp + 3.0) * ((NT - 1.0) / 6.0), 0.0, NT - 1.0)  36.2 us
    add x30, other arithmetic, downward(): source = planck_emission_factor[:, None] * (1.0 + 0.25 * layer[0][None, :])  36.1 us
    all_gather x1, blocking collectives, on_device(): lax.all_gather(own_hosts[None], 'gx', axis=0, tiled=True)  20.2 us
    all_gather x1, blocking collectives, on_device(): lax.all_gather(light[None], 'gx', axis=0, tiled=True)  17.3 us
  transfers between devices with their start and end apart: 6, of which 4 were waited for; matrix products, arithmetic and copies ran while one was open for 3% of the time, Pallas kernels for 0%

commit v1 on v0

v1 whole, which is shorter than its diff:
```python
import jax
import jax.numpy as jnp
from jax import lax
from jax.experimental import pallas as pl
from jax.experimental.pallas import tpu as pltpu
from jax.sharding import PartitionSpec as P

CAP = 4
NHOST = 16
L=30; G=140; GP=144; NT=16; NQ=8; R=32; X=128; NC=9
LOG2E=1.4426950408889634
DIFF=1.66
f32=jnp.float32; bf16=jnp.bfloat16
W2=2*X

diffusion = 0.2

def extended(block, sides, width):
    for axis, dim in sides:
        count = lax.axis_size(axis)
        forward = [(i, i + 1) for i in range(count - 1)]
        backward = [(target, source) for source, target in forward]
        low = lax.ppermute(
            lax.slice_in_dim(block, block.shape[dim] - width, None, axis=dim), axis, forward
        )
        high = lax.ppermute(lax.slice_in_dim(block, 0, width, axis=dim), axis, backward)
        block = jnp.concatenate([low, block, high], axis=dim)
    return block


def stencil(bordered_grid):
    centre = bordered_grid[:, :, 1:-1, 1:-1]
    beside_all = (
        bordered_grid[:, :, 2:, 1:-1]
        + bordered_grid[:, :, :-2, 1:-1]
        + bordered_grid[:, :, 1:-1, 2:]
        + bordered_grid[:, :, 1:-1, :-2]
    )
    return centre + diffusion * (beside_all - 4.0 * centre)


def make(thpre=True, dotbf=False, pstore=True, pairs=16, kext=True, wbf=False, lev=1):
    KW=144 if kext else 128
    def kernel(t_ref,q_ref,c_ref,sun_ref,lit_ref,tab_ref,cond_ref,pl_ref,ins_ref, heat_ref,surf_ref,
               hp,cb,ss,ds,th,tabs,pg,qg,cg,tr,pd,zacc,bacc,hk):
        K=-DIFF*LOG2E
        ri=lax.broadcasted_iota(jnp.int32,(GP,G),0); ci=lax.broadcasted_iota(jnp.int32,(GP,G),1)
        eye=ri==ci
        def col(ref):
            return jnp.sum(jnp.where(eye,ref[...],0.0),axis=1,keepdims=True)
        pcol=col(pl_ref); qcol=col(ins_ref); ccol=col(cond_ref)*K
        psum=jnp.sum(pl_ref[...]); qsum=jnp.sum(ins_ref[...])
        pg[...]=jnp.broadcast_to(pcol,(GP,X)).astype(bf16)
        qg[...]=jnp.broadcast_to(qcol,(GP,X))
        lane=lax.broadcasted_iota(jnp.int32,(GP,16),1)
        chi=ccol.astype(bf16).astype(f32)
        cext=jnp.where(lane==0,chi,jnp.where(lane==1,ccol-chi,0.0)).astype(bf16)
        def prep(l,_):
            tabs[l,:,0:128]=jnp.concatenate([tab_ref[l].astype(f32)*K,jnp.zeros((GP-G,128),f32)],axis=0).astype(bf16)
            if kext: tabs[l,:,128:144]=cext
            t=t_ref[l].astype(bf16).astype(f32)
            tp=jnp.clip((t+3.0)*((NT-1.0)/6.0),0.0,NT-1.0)
            for i in range(NT):
                th[l,i]=jnp.maximum(0.0,1.0-jnp.abs(tp-float(i)))
            s=1.0+0.25*t
            ss[l]=s
            hp[l]=jnp.clip(q_ref[l].astype(bf16).astype(f32)*(NQ-1.0),0.0,NQ-1.0)
            cb[l]=c_ref[l].astype(bf16).astype(f32)
            return 0
        lax.fori_loop(0,L,prep,0)
        s=ss[...]
        ds[0:L-1]=s[:-1]-s[1:]
        i8=lax.broadcasted_iota(jnp.int32,(NQ,W2),0).astype(f32)
        ex=(lax.broadcasted_iota(jnp.int32,(16,W2),0)<2).astype(f32)
        lr=lax.broadcasted_iota(jnp.int32,(32,480),0); lc=lax.broadcasted_iota(jnp.int32,(32,480),1)>>4
        selz=jnp.where(lr==30,(lc==29).astype(f32),(lc==lr-1).astype(f32)-(lc==lr).astype(f32)).astype(bf16)
        selb=jnp.where(lr<30,(lc==lr+1).astype(f32)-(lc==lr).astype(f32),0.0).astype(bf16)
        def tree(v):
            ws=[v[16*i:16*i+16] for i in range(NC)]
            while len(ws)>1:
                ws=[a+b for a,b in zip(ws[0::2],ws[1::2])]+([ws[-1]] if len(ws)%2 else [])
            return ws[0]
        def pair(p,_):
            r0=2*p
            def row(ref,*l):
                return jnp.concatenate([ref[(*l,pl.ds(r0,1),slice(None))],ref[(*l,pl.ds(r0+1,1),slice(None))]],axis=1)
            sun=row(sun_ref)
            lit=jnp.concatenate([jnp.full((1,X),lit_ref[0,r0].astype(f32)),jnp.full((1,X),lit_ref[0,r0+1].astype(f32))],axis=1)
            mu=sun.astype(bf16).astype(f32)
            inv=((1.0/DIFF)/mu).astype(bf16)
            light=(sun*lit).astype(bf16).astype(f32)
            P=jnp.concatenate([pg[...],pg[...]],axis=1)
            E=-(P*row(ss,0).astype(bf16))
            S=(jnp.concatenate([qg[...],qg[...]],axis=1)*light).astype(bf16)
            def depth(l):
                hh=jnp.maximum(0.0,1.0-jnp.abs(row(hp,l)-i8))
                W=[row(th,l,i)*hh for i in range(NT)]
                W=[jnp.concatenate(W[2*i:2*i+2],axis=0).astype(bf16) for i in range(NT//2)]
                if kext: W.append((ex*row(cb,l)).astype(bf16))
                W=jnp.concatenate(W,axis=0)
                x=jnp.dot(tabs[l],W,preferred_element_type=bf16 if dotbf else f32)
                return x.astype(bf16)
            for l in range(L):
                x=depth(l)
                trl=jnp.exp2(x)
                tr[l]=trl
                ts=jnp.exp2(x*inv)
                Xl=trl*E
                S=S*ts
                zacc[16*l:16*l+16]=tree(Xl+S)
                if l<L-1:
                    pds=P*row(ds,l).astype(bf16)
                    if pstore: pd[l]=pds
                    E=Xl+pds
            F=jnp.zeros((GP,W2),bf16)
            for l in range(L-1,-1,-1):
                Y=tr[l]*F if l<L-1 else F
                bacc[16*l:16*l+16]=tree(Y) if l<L-1 else jnp.zeros((16,W2),bf16)
                if l>0:
                    pds=pd[l-1] if pstore else P*row(ds,l-1).astype(bf16)
                    F=Y-pds
            h=jnp.dot(selz,zacc[...],preferred_element_type=f32)+jnp.dot(selb,bacc[...],preferred_element_type=f32)
            for k in range(2):
                hk[pl.ds(r0+k,32,stride=32),:]=h[:,X*k:X*k+X]
            return 0
        lax.fori_loop(0,pairs,pair,0)
        for l in range(L):
            g=hk[32*l:32*l+32]
            if l==0: g=g-psum*ss[0]
            else: g=g+psum*ds[l-1]
            if l<L-1: g=g-psum*ds[l]
            heat_ref[l]=g*(2.0/G)
        def lrow(r,_):
            li=(sun_ref[pl.ds(r,1),:]*lit_ref[0,r].astype(f32)).astype(bf16).astype(f32)
            heat_ref[0,pl.ds(r,1),:]=heat_ref[0,pl.ds(r,1),:]+qsum*(2.0/G)*li
            return 0
        lax.fori_loop(0,R,lrow,0)
        surf_ref[...]=(hk[32*30:32*31]+psum*ss[L-1])*(1.0/G)
    def run(t,q,c,sun,lit,table,cond,planck,insol):
        V=pltpu.VMEM
        fld=V((L,R,X),f32)
        vm=pl.BlockSpec(memory_space=pltpu.VMEM)
        return pl.pallas_call(kernel,out_shape=(jax.ShapeDtypeStruct((L,R,X),f32),jax.ShapeDtypeStruct((R,X),f32)),
            in_specs=[vm]*4+[pl.BlockSpec(memory_space=pltpu.SMEM)]+[vm]*4,
            scratch_shapes=[fld,fld,fld,fld,V((L,NT,R,X),f32),V((L,GP,KW),bf16),V((GP,X),bf16),V((GP,X),f32),V((GP,X),f32),
              V((L,GP,W2),bf16),V((L,GP,W2),bf16),V((480,W2),bf16),V((480,W2),bf16),V((1024,X),f32)],
            compiler_params=pltpu.CompilerParams(vmem_limit_bytes=56*2**20),
            )(t,q,c,sun,lit.reshape(1,R),table,cond.reshape(1,G),planck.reshape(1,G),insol.reshape(1,G))
    return run


def on_device(t, q, c, sun, lit, owner, table, cond, planck, insol):
    bordered = extended(jnp.stack((t, q)), (("gx", 3), ("gy", 2)), 1)
    blurred = stencil(bordered)
    heat, surf = make()(t, q, c, sun, lit[0], table, cond, planck, insol)
    own = owner[0, :, 0]
    earlier = jnp.arange(R)[None, :] < jnp.arange(R)[:, None]
    rank = jnp.sum(jnp.logical_and(own[:, None] == own[None, :], earlier), axis=1)
    place = own * CAP + rank
    pick = (place[None, :] == jnp.arange(NHOST * CAP)[:, None]).astype(f32)
    slots = jnp.dot(pick, surf, precision=lax.Precision.HIGHEST).reshape(NHOST, CAP, X)
    got = lax.all_to_all(slots, "gx", split_axis=0, concat_axis=0, tiled=True)
    return blurred[0] + heat, blurred[1], got[None, None]

def solution(mesh):
    placed = (
        P(None, "gy", "gx"),
        P(None, "gy", "gx"),
        P(None, "gy", "gx"),
        P("gy", "gx"),
        P("gx", "gy"),
        P("gx", "gy", None),
        P(),
        P(),
        P(),
        P(),
    )
    return jax.shard_map(
        on_device,
        mesh=mesh,
        in_specs=placed,
        out_specs=(P(None, "gy", "gx"), P(None, "gy", "gx"), P("gy", "gx", None, None, None)),
        check_vma=False,
    )
```

time: 645 us -> 76.6 us (0.12)
  matrix products: 423 us -> 0.14 us
  other arithmetic: 97.6 us -> 4.8 us
  Pallas kernels: 0 us -> 40.8 us
  blocking collectives: 37.5 us -> 11.9 us
  local copies, waits for them, and re-layouts: 27.6 us -> 3.84 us
  waiting for transfers between devices: 23 us -> 0.01 us
  between operations: 14.4 us -> 0.74 us
    dot_general x62 -> x1, matrix products: 423 us -> 0.14 us  [on_device(): jnp.dot(pick, surf, precision=lax.Precision.HIGHEST).reshape(NHOST, CAP, X)]
    pallas_call x0 -> x1, Pallas kernels: none -> 40.8 us  [run(): pl.pallas_call(kernel, out_shape=(jax.ShapeDtypeStruct((L, R, X), f32), j...]
    all_gather x2 -> x0, blocking collectives: 37.5 us -> none  [the longest x1 20.2 us: on_device(): lax.all_gather(own_hosts[None], 'gx', axis=0, tiled=True)]
    min x30 -> x0, other arithmetic: 36.2 us -> none  [optical_depth(): temp_pos = jnp.clip((air_temp + 3.0) * ((NT - 1.0) / 6.0), 0.0, NT - 1.0)]
    add x32 -> x2, other arithmetic: 36.2 us -> 0.86 us  [the longest x1 0.85 us: on_device(): return (blurred[0] + heat, blurred[1], got[None, None])]
    all_to_all x0 -> x1, blocking collectives: none -> 11.9 us  [on_device(): got = lax.all_to_all(slots, 'gx', split_axis=0, concat_axis=0, tiled=True)]
    all_gather x1 -> x0, waiting for transfers between devices: 11.5 us -> none  [on_device(): lax.all_gather(prognostic_bundle[None], 'gx', axis=0, tiled=True)]
    dynamic_update_slice x60 -> x0, local copies, waits for them, and re-layouts: 8.43 us -> none  [column_physics(): lax.scan(downward, (start_long, start_short), (layers, molecular_opacity_...]
  transfers between devices with their start and end apart: 6 -> 4, of which waited for: 4 -> 0; matrix products, arithmetic and copies ran while one was open for 3% -> 2% of each run, Pallas kernels for 0% -> 54%
where the time goes in v1:
time: 76.6 us; the launch traced here: 76.2 us
  Pallas kernels  40.8 us (53%)
  starting transfers between devices  14 us (18%)
  blocking collectives  11.9 us (16%)
  other arithmetic  4.8 us (6%)
  local copies, waits for them, and re-layouts  3.84 us (5%)
    pallas_call x1, Pallas kernels, run(): pl.pallas_call(kernel, out_shape=(jax.ShapeDtypeStruct((L, R, X), f32), j...  40.8 us
    all_to_all x1, blocking collectives, on_device(): got = lax.all_to_all(slots, 'gx', split_axis=0, concat_axis=0, tiled=True)  11.9 us
    ppermute x2, starting transfers between devices, extended(): lax.ppermute(lax.slice_in_dim(block, block.shape[dim] - width, None, axis...  10.8 us
    ppermute x2, starting transfers between devices, extended(): lax.ppermute(lax.slice_in_dim(block, 0, width, axis=dim), axis, backward)  3.21 us
    another operation x1, other arithmetic, on_device(): bordered = extended(jnp.stack((t, q)), (('gx', 3), ('gy', 2)), 1)  1.84 us
  transfers between devices with their start and end apart: 4, of which 0 were waited for; matrix products, arithmetic and copies ran while one was open for 2% of the time, Pallas kernels for 54%

profile of v1, /device:TPU:1, one launch (start us, length us, event | category | flops | bytes accessed | tf_op | source)
XLA Modules:
  0.0 76.2 jit_solution(3625138282782953493)
XLA Ops:
  0.6 1.8 %fusion.1 = (f32[2,30,32,1]{3,2,1,0:T(8,128)S(1)}, f32[2,30,32,1]{3,2,1,0:T(8,128)S(1)}) fusion(f32[1,30,32,128]{3,2,1,0:T(8,128)} %bitcast.16, f32[1,30,32,128]{3,2,1,0:T(8,128)} %bitcast.19), kind=kLoop, calls=%fused_computation.6 | loop fusion | flops 3840 | bytes 998400 | tf_op jit(solution)/shard_map/stack | solution.py:153
  2.5 0.0 copy-start.4
  2.5 0.4 copy.19
  2.9 4.9 %collective-permute-start = (f32[2,30,32,1]{2,0,3,1:T(2,128)S(1)}, f32[2,30,32,1]{2,0,3,1:T(2,128)S(1)}, u32[]{:S(2)}, u32[]{:S(2)}) collective-permute-start(f32[2,30,32,1]{2,0,3,1:T(2,128)S(1)} %copy.19), channel_id=1, source_target_pairs={{0,8},{8,16},{16,24},{24,32},{32,40},{40,48},{48,56},{56,64},{64,7... | collective-permute-start | bytes 23048 | tf_op jit(solution)/shard_map/ppermute | solution.py:23
  7.9 0.4 copy.20
  8.3 1.9 %collective-permute-start.1 = (f32[2,30,32,1]{2,0,3,1:T(2,128)S(1)}, f32[2,30,32,1]{2,0,3,1:T(2,128)S(1)}, u32[]{:S(2)}, u32[]{:S(2)}) collective-permute-start(f32[2,30,32,1]{2,0,3,1:T(2,128)S(1)} %copy.20), channel_id=1, source_target_pairs={{8,0},{16,8},{24,16},{32,24},{40,32},{48,40},{56,48},{64,56},{72,6... | collective-permute-start | bytes 23048 | tf_op jit(solution)/shard_map/ppermute | solution.py:26
  10.2 0.2 convert_reduce_fusion
  10.4 40.8 %shard_map.121 = (f32[30,32,128]{2,1,0:T(8,128)}, f32[32,128]{1,0:T(8,128)}) custom-call(f32[30,32,128]{2,1,0:T(8,128)} %t_ref.1, f32[30,32,128]{2,1,0:T(8,128)} %q_ref.1, f32[30,32,128]{2,1,0:T(8,128)} %c_ref.1, f32[32,128]{1,0:T(8,128)} %sun_ref.1, s32[1,32]{1,0:T(1,128)} %lit_ref.1, bf16[30,140,128]{2,1,0:T(8,128)(2,1)} %tab_ref.1, f32[1,140]{1,0:T(1,128)} %bitcast.24, ...), custom_call_target="tpu_custom_call" | custom-call | tf_op jit(solution)/shard_map/pallas_call | solution.py:143
  51.2 0.0 collective-permute-done
  51.2 0.4 copy.21
  51.7 0.4 copy.22
  52.1 0.1 copy-done
  52.2 0.1 copy-done.1
  52.4 0.4 pad_maximum_fusion.16
  52.8 1.3 %collective-permute-start.2 = (f32[2,30,1,130]{3,2,1,0:T(1,128)S(1)}, f32[2,30,1,130]{3,2,1,0:T(1,128)S(1)}, u32[]{:S(2)}, u32[]{:S(2)}) collective-permute-start(f32[2,30,1,130]{3,2,1,0:T(1,128)S(1)} %get-tuple-element.7), channel_id=1, source_target_pairs={{1,0},{2,1},{3,2},{4,3},{5,4},{6,5},{7,6},{9,8},{10,9},{11,10},{12... | collective-permute-start | bytes 93608 | tf_op jit(solution)/shard_map/ppermute | solution.py:26
  54.1 5.8 %collective-permute-start.3 = (f32[2,30,1,130]{3,2,1,0:T(1,128)S(1)}, f32[2,30,1,130]{3,2,1,0:T(1,128)S(1)}, u32[]{:S(2)}, u32[]{:S(2)}) collective-permute-start(f32[2,30,1,130]{3,2,1,0:T(1,128)S(1)} %get-tuple-element.8), channel_id=1, source_target_pairs={{0,1},{1,2},{2,3},{3,4},{4,5},{5,6},{6,7},{8,9},{9,10},{10,11},{11... | collective-permute-start | bytes 93608 | tf_op jit(solution)/shard_map/ppermute | solution.py:23
  60.0 0.1 fusion.9
  60.1 11.9 %all_to_all.5 = f32[16,4,128]{2,1,0:T(4,128)S(1)} all-to-all(f32[16,4,128]{2,1,0:T(4,128)S(1)} %bitcast.23), channel_id=1, replica_groups=mesh['gx'=16,'gy'=8] {'gx'}, dimensions={0} | all-to-all | bytes 65536 | tf_op jit(solution)/shard_map/all_to_all | solution.py:162
  72.0 1.5 %fusion.5 = f32[2,30,32,128]{3,2,1,0:T(8,128)S(1)} fusion(f32[2,30,32,1]{3,2,1,0:T(8,128)S(1)} %copy.21, f32[1,30,32,128]{3,2,1,0:T(8,128)S(1)} %bitcast.21, f32[1,30,32,128]{3,2,1,0:T(8,128)S(1)} %bitcast.18, f32[2,30,32,1]{3,2,1,0:T(8,128)S(1)} %copy.22, f32[2,30,1,130]{3,2,1,0:T(1,128)S(1)} %collective-permute-done.3, ...), kind=kLoop, calls=%fused_computation.11 | loop fusion | flops 4915200 | bytes 2043840 | tf_op jit(solution)/shard_map/add | solution.py:39
  73.5 0.0 copy-start.2
  73.5 0.8 %slice_bitcast_fusion = f32[30,32,128]{2,1,0:T(8,128)} fusion(f32[2,30,32,128]{3,2,1,0:T(8,128)S(1)} %fusion.5), kind=kLoop, calls=%fused_computation.25 | loop fusion | bytes 983040 | tf_op jit(solution)/shard_map/squeeze | solution.py:163
  74.3 0.4 copy-done.2
  74.7 0.9 %fusion.8 = f32[30,32,128]{2,1,0:T(8,128)} fusion(f32[30,32,128]{2,1,0:T(8,128)S(1)} %copy-done.2, f32[2,30,32,128]{3,2,1,0:T(8,128)S(1)} %fusion.5), kind=kLoop, calls=%fused_computation.27 | loop fusion | flops 122880 | bytes 1474560 | tf_op jit(solution)/shard_map/add | solution.py:163
  75.6 0.6 copy.26
  (9 shorter events, 0.0 us)
Async XLA Ops:
  2.5 7.7 %copy-start.4 = (s32[1,32,1]{1,2,0:T(1,128)S(1)}, s32[1,32,1]{1,2,0:T(1,128)}, u32[]{:S(2)}) copy-start(s32[1,32,1]{1,2,0:T(1,128)} %param.15) | copy-start | bytes 388
  2.9 48.3 %collective-permute-start = (f32[2,30,32,1]{2,0,3,1:T(2,128)S(1)}, f32[2,30,32,1]{2,0,3,1:T(2,128)S(1)}, u32[]{:S(2)}, u32[]{:S(2)}) collective-permute-start(f32[2,30,32,1]{2,0,3,1:T(2,128)S(1)} %copy.19), channel_id=1, source_target_pairs={{0,8},{8,16},{16,24},{24,32},{32,40},{40,48},{48,56},{56,64},{64,7... | collective-permute-start | bytes 23048 | tf_op jit(solution)/shard_map/ppermute | solution.py:23
  8.3 43.4 %collective-permute-start.1 = (f32[2,30,32,1]{2,0,3,1:T(2,128)S(1)}, f32[2,30,32,1]{2,0,3,1:T(2,128)S(1)}, u32[]{:S(2)}, u32[]{:S(2)}) collective-permute-start(f32[2,30,32,1]{2,0,3,1:T(2,128)S(1)} %copy.20), channel_id=1, source_target_pairs={{8,0},{16,8},{24,16},{32,24},{40,32},{48,40},{56,48},{64,56},{72,6... | collective-permute-start | bytes 23048 | tf_op jit(solution)/shard_map/ppermute | solution.py:26
  51.2 1.0 %copy-start = (f32[30,32,128]{2,1,0:T(8,128)S(1)}, f32[30,32,128]{2,1,0:T(8,128)}, u32[]{:S(2)}) copy-start(f32[30,32,128]{2,1,0:T(8,128)} %t_ref.1) | copy-start | bytes 1474564
  51.2 1.2 %copy-start.1 = (f32[30,32,128]{2,1,0:T(8,128)S(1)}, f32[30,32,128]{2,1,0:T(8,128)}, u32[]{:S(2)}) copy-start(f32[30,32,128]{2,1,0:T(8,128)} %q_ref.1) | copy-start | bytes 1474564
  52.4 7.6 %copy-start.3 = (f32[32,128]{1,0:T(8,128)S(1)}, f32[32,128]{1,0:T(8,128)}, u32[]{:S(2)}) copy-start(f32[32,128]{1,0:T(8,128)} %get-tuple-element.6) | copy-start | bytes 49156
  52.8 19.2 %collective-permute-start.2 = (f32[2,30,1,130]{3,2,1,0:T(1,128)S(1)}, f32[2,30,1,130]{3,2,1,0:T(1,128)S(1)}, u32[]{:S(2)}, u32[]{:S(2)}) collective-permute-start(f32[2,30,1,130]{3,2,1,0:T(1,128)S(1)} %get-tuple-element.7), channel_id=1, source_target_pairs={{1,0},{2,1},{3,2},{4,3},{5,4},{6,5},{7,6},{9,8},{10,9},{11,10},{12... | collective-permute-start | bytes 93608 | tf_op jit(solution)/shard_map/ppermute | solution.py:26
  54.1 17.9 %collective-permute-start.3 = (f32[2,30,1,130]{3,2,1,0:T(1,128)S(1)}, f32[2,30,1,130]{3,2,1,0:T(1,128)S(1)}, u32[]{:S(2)}, u32[]{:S(2)}) collective-permute-start(f32[2,30,1,130]{3,2,1,0:T(1,128)S(1)} %get-tuple-element.8), channel_id=1, source_target_pairs={{0,1},{1,2},{2,3},{3,4},{4,5},{5,6},{6,7},{8,9},{9,10},{10,11},{11... | collective-permute-start | bytes 93608 | tf_op jit(solution)/shard_map/ppermute | solution.py:23
  73.5 1.2 %copy-start.2 = (f32[30,32,128]{2,1,0:T(8,128)S(1)}, f32[30,32,128]{2,1,0:T(8,128)}, u32[]{:S(2)}) copy-start(f32[30,32,128]{2,1,0:T(8,128)} %get-tuple-element.5) | copy-start | bytes 1474564

commit v2 on v1

v2 whole, which is shorter than its diff:
```python
import jax
import jax.numpy as jnp
from jax import lax
from jax.experimental import pallas as pl
from jax.experimental.pallas import tpu as pltpu
from jax.sharding import PartitionSpec as P

L, G, GP, NT, NQ, R, X = 30, 140, 144, 16, 8, 32, 128
NC = GP // 16
KW = 144
W2 = 2 * X
PAIRS = R // 2
CAP = 4
N_GX, N_GY = 16, 8
CH = 5
NK = L // CH
diffusion = 0.2
diffusivity = 1.66
SCALE = -diffusivity * 1.4426950408889634
f32, bf16 = jnp.float32, jnp.bfloat16


def kernel(
    t_ref, q_ref, c_ref, sun_ref, lit_ref, own_ref, tab_ref, cond_ref, planck_ref, insol_ref,
    adv_ref, hum_ref, slot_ref,
    hp, cb, ss, ds, th, tabs, pg, qg, tr_a, tr_b, pd_a, pd_b, zacc, bacc, hk, hz, inc, sf,
    xb, Es, Ss, Fs, iv, nsend, nrecv, esend, erecv, ssend, srecv,
    halo_out, halo_in, slot_out, slot_in,
):
    gx, gy = lax.axis_index("gx"), lax.axis_index("gy")
    barrier = pltpu.get_barrier_semaphore()
    mates = [{"gx": lax.rem(gx + d, N_GX), "gy": gy} for d in range(1, N_GX)]
    beside = [{"gx": gx, "gy": lax.rem(gy + d, N_GY)} for d in (1, N_GY - 1)]
    for one_device in mates + beside:
        pl.semaphore_signal(barrier, inc=1, device_id=one_device, device_id_type=pl.DeviceIdType.MESH)

    trs, pds = (tr_a, tr_b), (pd_a, pd_b)

    eye = lax.broadcasted_iota(jnp.int32, (GP, G), 0) == lax.broadcasted_iota(jnp.int32, (GP, G), 1)

    def column(ref):
        return jnp.sum(jnp.where(eye, ref[...], 0.0), axis=1, keepdims=True)

    ccol = column(cond_ref) * SCALE
    psum, qsum = jnp.sum(planck_ref[...]), jnp.sum(insol_ref[...])
    pg[...] = jnp.broadcast_to(column(planck_ref), (GP, X)).astype(bf16)
    qg[...] = jnp.broadcast_to(column(insol_ref), (GP, X))
    lane16 = lax.broadcasted_iota(jnp.int32, (GP, 16), 1)
    chi = ccol.astype(bf16).astype(f32)
    cext = jnp.where(lane16 == 0, chi, jnp.where(lane16 == 1, ccol - chi, 0.0)).astype(bf16)
    lane = lax.broadcasted_iota(jnp.int32, (R, X), 1)
    line = lax.broadcasted_iota(jnp.int32, (R, X), 0)
    nsend[...] = jnp.zeros_like(nsend)
    ds[0] = jnp.zeros((R, X), f32)

    def prepare(l, edges):
        tabs[l, :, 0:NT * NQ] = jnp.concatenate(
            [tab_ref[l].astype(f32) * SCALE, jnp.zeros((GP - G, NT * NQ), f32)], axis=0
        ).astype(bf16)
        tabs[l, :, NT * NQ:KW] = cext
        warm, wet = t_ref[l], q_ref[l]
        t = warm.astype(bf16).astype(f32)
        tp = jnp.clip((t + 3.0) * ((NT - 1.0) / 6.0), 0.0, NT - 1.0)
        for i in range(NT):
            th[l, i] = jnp.maximum(0.0, 1.0 - jnp.abs(tp - float(i)))
        s = 1.0 + 0.25 * t
        ss[l] = s
        ds[l] = edges[4] - s
        hp[l] = jnp.clip(wet.astype(bf16).astype(f32) * (NQ - 1.0), 0.0, NQ - 1.0)
        cb[l] = c_ref[l].astype(bf16).astype(f32)
        here = lane == l
        out = []
        for field, v in enumerate((warm, wet)):
            nsend[0, field, pl.ds(l, 1), :] = v[0:1]
            nsend[1, field, pl.ds(l, 1), :] = v[R - 1:R]
            out.append(jnp.where(here, pltpu.roll(v, l, 1), edges[2 * field]))
            out.append(jnp.where(here, pltpu.roll(v, l + 1, 1), edges[2 * field + 1]))
        return tuple(out) + (s,)

    none = jnp.zeros((R, X), f32)
    edges = lax.fori_loop(0, L, prepare, (none,) * 5)
    ds[L] = none
    for field in range(2):
        for side in range(2):
            esend[side, field] = edges[2 * field + side]

    pl.semaphore_wait(barrier, N_GX + 1)
    west, east = {"gx": lax.rem(gx + N_GX - 1, N_GX), "gy": gy}, {"gx": lax.rem(gx + 1, N_GX), "gy": gy}
    south, north = {"gx": gx, "gy": lax.rem(gy + N_GY - 1, N_GY)}, {"gx": gx, "gy": lax.rem(gy + 1, N_GY)}
    halos = []
    for n, (src, dst, target) in enumerate((
        (esend.at[0], erecv.at[1], west), (esend.at[1], erecv.at[0], east),
        (nsend.at[0], nrecv.at[1], south), (nsend.at[1], nrecv.at[0], north),
    )):
        halos.append(pltpu.make_async_remote_copy(
            src_ref=src, dst_ref=dst, send_sem=halo_out.at[n], recv_sem=halo_in.at[n],
            device_id=target, device_id_type=pl.DeviceIdType.MESH,
        ))
        halos[-1].start()

    i8 = lax.broadcasted_iota(jnp.int32, (NQ, W2), 0).astype(f32)
    ex = (lax.broadcasted_iota(jnp.int32, (16, W2), 0) < 2).astype(f32)
    lr = lax.broadcasted_iota(jnp.int32, (32, 16 * L), 0)
    lc = lax.broadcasted_iota(jnp.int32, (32, 16 * L), 1) >> 4
    selz = jnp.where(
        lr == L, (lc == L - 1).astype(f32), (lc == lr - 1).astype(f32) - (lc == lr).astype(f32)
    ).astype(bf16)
    selb = jnp.where(lr < L, (lc == lr + 1).astype(f32) - (lc == lr).astype(f32), 0.0).astype(bf16)

    def tree(v):
        parts = [v[16 * i:16 * i + 16] for i in range(NC)]
        while len(parts) > 1:
            parts = [a + b for a, b in zip(parts[0::2], parts[1::2])] + (
                [parts[-1]] if len(parts) % 2 else []
            )
        return parts[0]

    def row(ref, r0, *at):
        return jnp.concatenate(
            [ref[(*at, pl.ds(r0, 1), slice(None))], ref[(*at, pl.ds(r0 + 1, 1), slice(None))]], axis=1
        )

    def both(v):
        return jnp.concatenate([v, v], axis=1)

    def depth(p, l, j):
        r0 = 2 * p
        hh = jnp.maximum(0.0, 1.0 - jnp.abs(row(hp, r0, l) - i8))
        w = [row(th, r0, l, i) * hh for i in range(NT)]
        w = [jnp.concatenate(w[2 * i:2 * i + 2], axis=0).astype(bf16) for i in range(NT // 2)]
        w.append((ex * row(cb, r0, l)).astype(bf16))
        xb[j] = jnp.dot(
            tabs[l], jnp.concatenate(w, axis=0), preferred_element_type=f32
        ).astype(bf16)

    def start(p):
        r0 = 2 * p
        sun = row(sun_ref, r0)
        lit = jnp.concatenate(
            [jnp.full((1, X), lit_ref[0, r0 + k].astype(f32)) for k in range(2)], axis=1
        )
        iv[...] = jnp.broadcast_to(
            (1.0 / diffusivity) / sun.astype(bf16).astype(f32), (16, W2)
        ).astype(bf16)
        light = (sun * lit).astype(bf16).astype(f32)
        for k in range(2):
            inc[pl.ds(r0 + k, 1), :] = light[:, X * k:X * k + X]
        Es[...] = both(pg[...]) * row(ds, r0, 0).astype(bf16)
        Ss[...] = (both(qg[...]) * light).astype(bf16)

    def down(p, k, par):
        r0 = 2 * p
        E, S = Es[...], Ss[...]
        inv = jnp.concatenate([iv[...]] * NC, axis=0)
        for j in range(CH):
            l = k * CH + j
            x = xb[j]
            trl = jnp.exp2(x)
            trs[par][l] = trl
            down_part = trl * E
            S = S * jnp.exp2(x * inv)
            zacc[l] = tree(down_part + S)
            step = both(pg[...]) * row(ds, r0, l + 1).astype(bf16)
            pds[par][l + 1] = step
            E = down_part + step
        Es[...] = E
        Ss[...] = S

    def up(k, par):
        F = Fs[...]
        for j in range(CH):
            l = L - 1 - (k * CH + j)
            up_part = trs[par][l] * F
            bacc[l] = tree(up_part)
            F = up_part - pds[par][l]
        Fs[...] = F

    def down_sums(p):
        h = jnp.dot(selz, zacc[...].reshape(16 * L, W2), preferred_element_type=f32)
        hz[...] = h
        for k in range(2):
            sf[pl.ds(2 * p + k, 1), :] = h[L:L + 1, X * k:X * k + X]

    def up_sums(p):
        h = hz[...] + jnp.dot(selb, bacc[...].reshape(16 * L, W2), preferred_element_type=f32)
        for k in range(2):
            hk[pl.ds(2 * p + k, 32, stride=32), :] = h[:, X * k:X * k + X]

    def chunks(body):
        def step(k, carry):
            body(k)
            return carry

        lax.fori_loop(0, NK, step, 0)

    def next_and_down(p, k, par):
        n = p * NK + k + 1
        pn, kn = lax.rem(lax.div(n, NK), PAIRS), lax.rem(n, NK)
        down(p, k, par)
        for j in range(CH):
            depth(pn, kn * CH + j, j)

    def whole(p, par):
        start(p)
        Fs[...] = jnp.zeros((GP, W2), bf16)

        def body(k):
            up(k, 1 - par)
            next_and_down(p, k, par)

        chunks(body)
        up_sums(p - 1)
        down_sums(p)

    for ref in pds:
        ref[0] = jnp.zeros((GP, W2), bf16)
    for j in range(CH):
        depth(0, j, j)
    start(0)
    chunks(lambda k: next_and_down(0, k, 0))
    down_sums(0)

    def two(i, carry):
        whole(2 * i + 1, 1)
        whole(2 * i + 2, 0)
        return carry

    lax.fori_loop(0, (PAIRS - 2) // 2, two, 0)
    whole(PAIRS - 1, 1)

    surface = (sf[...] + psum * ss[L - 1]) * (1.0 / G)
    own = own_ref[...].reshape(R, 1).astype(f32)
    er = lax.broadcasted_iota(jnp.int32, (R, R), 0)
    ec = lax.broadcasted_iota(jnp.int32, (R, R), 1)
    own_row = jnp.sum(jnp.where(er == ec, own, 0.0), axis=0, keepdims=True)
    rank = jnp.sum(
        jnp.where(jnp.logical_and(er < ec, own == own_row), 1.0, 0.0), axis=0, keepdims=True
    )
    pick = lax.broadcasted_iota(jnp.int32, (8 * N_GX, R), 0).astype(f32) == own_row * 8.0 + rank
    slots = jnp.dot(
        pick.astype(f32), surface, precision=lax.Precision.HIGHEST, preferred_element_type=f32
    )
    ssend[...] = slots.reshape(N_GX, 8, X)
    sends = []
    for d in range(1, N_GX):
        to = lax.rem(gx + d, N_GX)
        sends.append(pltpu.make_async_remote_copy(
            src_ref=ssend.at[to], dst_ref=srecv.at[gx], send_sem=slot_out.at[d],
            recv_sem=slot_in.at[d], device_id={"gx": to, "gy": gy},
            device_id_type=pl.DeviceIdType.MESH,
        ))
        sends[-1].start()

    Fs[...] = jnp.zeros((GP, W2), bf16)
    chunks(lambda k: up(k, 1))
    up_sums(PAIRS - 1)

    hk[0:R] = hk[0:R] + qsum * inc[...]
    for copy in halos:
        copy.wait()
    inside_w = (gx > 0).astype(f32)
    inside_e = (gx < N_GX - 1).astype(f32)
    inside_s = (gy > 0).astype(f32)
    inside_n = (gy < N_GY - 1).astype(f32)

    def smooth(l, field, v):
        low = jnp.where(line == 0, nrecv[0, field, pl.ds(l, 1), :] * inside_s, pltpu.roll(v, 1, 0))
        high = jnp.where(
            line == R - 1, nrecv[1, field, pl.ds(l, 1), :] * inside_n, pltpu.roll(v, R - 1, 0)
        )
        left = jnp.where(
            lane == 0, pltpu.roll(erecv[0, field], lax.rem(X - l, X), 1) * inside_w, pltpu.roll(v, 1, 1)
        )
        right = jnp.where(
            lane == X - 1, pltpu.roll(erecv[1, field], X - 1 - l, 1) * inside_e,
            pltpu.roll(v, X - 1, 1),
        )
        return v + diffusion * (low + high + left + right - 4.0 * v)

    def last(l, carry):
        gain = hk[pl.ds(pl.multiple_of(R * l, R), R), :] + psum * (ds[l] - ds[l + 1])
        adv_ref[l] = smooth(l, 0, t_ref[l]) + gain * (2.0 / G)
        hum_ref[l] = smooth(l, 1, q_ref[l])
        return carry

    lax.fori_loop(0, L, last, 0)
    for copy in sends:
        copy.wait()
    srecv[gx] = ssend[gx]
    slot_ref[...] = srecv[:, 0:CAP, :]


def on_device(t, q, c, sun, lit, owner, table, cond, planck, insol):
    vmem, scratch = pl.BlockSpec(memory_space=pltpu.VMEM), pltpu.VMEM
    field = scratch((L, R, X), f32)
    levels = scratch((L, GP, W2), bf16)
    state = scratch((GP, W2), bf16)
    out = pl.pallas_call(
        kernel,
        out_shape=(
            jax.ShapeDtypeStruct((L, R, X), f32),
            jax.ShapeDtypeStruct((L, R, X), f32),
            jax.ShapeDtypeStruct((N_GX, CAP, X), f32),
        ),
        in_specs=[vmem] * 4 + [pl.BlockSpec(memory_space=pltpu.SMEM)] + [vmem] * 5,
        out_specs=(vmem,) * 3,
        scratch_shapes=[
            field, field, field, scratch((L + 1, R, X), f32), scratch((L, NT, R, X), f32),
            scratch((L, GP, KW), bf16), scratch((GP, X), bf16), scratch((GP, X), f32),
            levels, levels, scratch((L + 1, GP, W2), bf16), scratch((L + 1, GP, W2), bf16),
            scratch((L, 16, W2), bf16), scratch((L, 16, W2), bf16),
            scratch((32 * R, X), f32), scratch((32, W2), f32), scratch((R, X), f32),
            scratch((R, X), f32), scratch((CH, GP, W2), bf16), state, state, state,
            scratch((16, W2), bf16),
            scratch((2, 2, R, X), f32), scratch((2, 2, R, X), f32),
            scratch((2, 2, R, X), f32), scratch((2, 2, R, X), f32),
            scratch((N_GX, 8, X), f32), scratch((N_GX, 8, X), f32),
            pltpu.SemaphoreType.DMA((4,)), pltpu.SemaphoreType.DMA((4,)),
            pltpu.SemaphoreType.DMA((N_GX,)), pltpu.SemaphoreType.DMA((N_GX,)),
        ],
        compiler_params=pltpu.CompilerParams(
            collective_id=0, has_side_effects=True, vmem_limit_bytes=56 * 2**20
        ),
    )(t, q, c, sun, lit, owner, table, cond[None], planck[None], insol[None])
    return out[0], out[1], out[2][None, None]


def solution(mesh):
    placed = (
        P(None, "gy", "gx"),
        P(None, "gy", "gx"),
        P(None, "gy", "gx"),
        P("gy", "gx"),
        P("gx", "gy"),
        P("gx", "gy", None),
        P(),
        P(),
        P(),
        P(),
    )
    return jax.shard_map(
        on_device,
        mesh=mesh,
        in_specs=placed,
        out_specs=(P(None, "gy", "gx"), P(None, "gy", "gx"), P("gy", "gx", None, None, None)),
        check_vma=False,
    )
```

time: 76.6 us -> 57.4 us (0.75)
  starting transfers between devices: 14 us -> 0 us
  blocking collectives: 11.9 us -> 0 us
  Pallas kernels: 40.8 us -> 51.9 us
  other arithmetic: 4.8 us -> 0 us
  local copies, waits for them, and re-layouts: 3.84 us -> 4.64 us
    ppermute x4 -> x0, starting transfers between devices: 14 us -> none  [the longest x2 10.8 us: extended(): lax.ppermute(lax.slice_in_dim(block, block.shape[dim] - width, None, axis...]
    all_to_all x1 -> x0, blocking collectives: 11.9 us -> none  [on_device(): got = lax.all_to_all(slots, 'gx', split_axis=0, concat_axis=0, tiled=True)]
    pallas_call x1, Pallas kernels: 40.8 us -> 51.9 us  [on_device(): pl.pallas_call(kernel, out_shape=(jax.ShapeDtypeStruct((L, R, X), f32), j...]
    unnamed x11 -> x8, local copies, waits for them, and re-layouts: 1.31 us -> 4.64 us
    add x3 -> x0, other arithmetic: 2.33 us -> none  [the longest x1 1.47 us: stencil(): return centre + diffusion * (beside_all - 4.0 * centre)]
    another operation x1 -> x0, other arithmetic: 1.84 us -> none  [on_device(): bordered = extended(jnp.stack((t, q)), (('gx', 3), ('gy', 2)), 1)]
    ppermute x2 -> x0, local copies, waits for them, and re-layouts: 0.87 us -> none  [the longest x1 0.43 us: extended(): lax.ppermute(lax.slice_in_dim(block, 0, width, axis=dim), axis, backward)]
    slice x2 -> x0, local copies, waits for them, and re-layouts: 0.85 us -> none  [the longest x1 0.43 us: extended(): lax.slice_in_dim(block, block.shape[dim] - width, None, axis=dim)]
  transfers between devices with their start and end apart: 4 -> 0, of which waited for: 0 -> 0; matrix products, arithmetic and copies ran while one was open for 2% -> 0% of each run, Pallas kernels for 54% -> 0%
where the time goes in v2:
time: 57.4 us; the launch traced here: 57.2 us
  Pallas kernels  51.9 us (90%)
  local copies, waits for them, and re-layouts  4.64 us (8%)
  between operations  0.66 us (1%)
    pallas_call x1, Pallas kernels, on_device(): pl.pallas_call(kernel, out_shape=(jax.ShapeDtypeStruct((L, R, X), f32), j...  51.9 us
    unnamed x8, local copies, waits for them, and re-layouts  4.64 us

profile of v2, /device:TPU:1, one launch (start us, length us, event | category | flops | bytes accessed | tf_op | source)
XLA Modules:
  0.0 57.2 jit_solution(16010623823313955755)
XLA Ops:
  0.6 1.3 %copy.13.own_ref = s32[1,32,1]{2,1,0:T(8,128)} copy(s32[1,32,1]{1,2,0:T(1,128)} %param.15) | data formatting | bytes 256 | tf_op args[5]
  2.0 51.9 %shard_map.121 = (f32[30,32,128]{2,1,0:T(8,128)}, f32[30,32,128]{2,1,0:T(8,128)}, f32[16,4,128]{2,1,0:T(4,128)}) custom-call(f32[30,32,128]{2,1,0:T(8,128)} %t_ref.1, f32[30,32,128]{2,1,0:T(8,128)} %q_ref.1, f32[30,32,128]{2,1,0:T(8,128)} %c_ref.1, f32[32,128]{1,0:T(8,128)} %sun_ref.1, s32[1,32]{1,0:T(1,128)} %lit_ref.1, s32[1,32,1]{2,1,0:T(8,128)} %copy.13.own_ref, ...), custom_call_target="tpu_custom_call" | custom-call | tf_op jit(solution)/shard_map/pallas_call | solution.py:298
  53.9 0.0 copy-start
  53.9 0.0 copy-start.1
  53.9 1.9 %copy.17 = f32[30,32,128]{2,1,0:T(8,128)} copy(f32[30,32,128]{2,1,0:T(8,128)} %get-tuple-element.12) | data formatting | bytes 983040
  55.8 0.0 copy-done
  55.8 0.8 %copy.18 = f32[30,32,128]{2,1,0:T(8,128)} copy(f32[30,32,128]{2,1,0:T(8,128)S(1)} %copy-done) | data formatting | bytes 983040
  56.6 0.0 copy-done.1
  56.6 0.6 %copy.19 = f32[1,1,16,4,128]{4,3,2,1,0:T(4,128)} copy(f32[1,1,16,4,128]{4,3,2,1,0:T(4,128)S(1)} %bitcast.4) | data formatting | bytes 65536
Async XLA Ops:
  53.9 1.9 %copy-start = (f32[30,32,128]{2,1,0:T(8,128)S(1)}, f32[30,32,128]{2,1,0:T(8,128)}, u32[]{:S(2)}) copy-start(f32[30,32,128]{2,1,0:T(8,128)} %get-tuple-element.13) | copy-start | bytes 1474564
  53.9 2.7 %copy-start.1 = (f32[16,4,128]{2,1,0:T(4,128)S(1)}, f32[16,4,128]{2,1,0:T(4,128)}, u32[]{:S(2)}) copy-start(f32[16,4,128]{2,1,0:T(4,128)} %get-tuple-element.8) | copy-start | bytes 98308

commit v3 on v2

--- a/solution.py
+++ b/solution.py
@@ -12,7 +12,7 @@
 PAIRS = R // 2
 CAP = 4
 N_GX, N_GY = 16, 8
-CH = 5
+CH = 10
 NK = L // CH
 diffusion = 0.2
 diffusivity = 1.66
@@ -21,8 +21,8 @@
 
 
 def kernel(
-    t_ref, q_ref, c_ref, sun_ref, lit_ref, own_ref, tab_ref, cond_ref, planck_ref, insol_ref,
-    adv_ref, hum_ref, slot_ref,
+    t_ref, q_ref, c_ref, sun_ref, lit_ref, place_ref, tab_ref, cond_ref, planck_ref, insol_ref,
+    gain_ref, halo_ref, slot_ref,
     hp, cb, ss, ds, th, tabs, pg, qg, tr_a, tr_b, pd_a, pd_b, zacc, bacc, hk, hz, inc, sf,
     xb, Es, Ss, Fs, iv, nsend, nrecv, esend, erecv, ssend, srecv,
     halo_out, halo_in, slot_out, slot_in,
@@ -49,7 +49,6 @@
     chi = ccol.astype(bf16).astype(f32)
     cext = jnp.where(lane16 == 0, chi, jnp.where(lane16 == 1, ccol - chi, 0.0)).astype(bf16)
     lane = lax.broadcasted_iota(jnp.int32, (R, X), 1)
-    line = lax.broadcasted_iota(jnp.int32, (R, X), 0)
     nsend[...] = jnp.zeros_like(nsend)
     ds[0] = jnp.zeros((R, X), f32)
 
@@ -229,14 +228,7 @@
     whole(PAIRS - 1, 1)
 
     surface = (sf[...] + psum * ss[L - 1]) * (1.0 / G)
-    own = own_ref[...].reshape(R, 1).astype(f32)
-    er = lax.broadcasted_iota(jnp.int32, (R, R), 0)
-    ec = lax.broadcasted_iota(jnp.int32, (R, R), 1)
-    own_row = jnp.sum(jnp.where(er == ec, own, 0.0), axis=0, keepdims=True)
-    rank = jnp.sum(
-        jnp.where(jnp.logical_and(er < ec, own == own_row), 1.0, 0.0), axis=0, keepdims=True
-    )
-    pick = lax.broadcasted_iota(jnp.int32, (8 * N_GX, R), 0).astype(f32) == own_row * 8.0 + rank
+    pick = lax.broadcasted_iota(jnp.int32, (8 * N_GX, R), 0).astype(f32) == place_ref[...]
     slots = jnp.dot(
         pick.astype(f32), surface, precision=lax.Precision.HIGHEST, preferred_element_type=f32
     )
@@ -256,38 +248,39 @@
     up_sums(PAIRS - 1)
 
     hk[0:R] = hk[0:R] + qsum * inc[...]
+    for l in range(L):
+        gain_ref[l] = (hk[R * l:R * l + R] + psum * (ds[l] - ds[l + 1])) * (2.0 / G)
     for copy in halos:
         copy.wait()
-    inside_w = (gx > 0).astype(f32)
-    inside_e = (gx < N_GX - 1).astype(f32)
-    inside_s = (gy > 0).astype(f32)
-    inside_n = (gy < N_GY - 1).astype(f32)
-
-    def smooth(l, field, v):
-        low = jnp.where(line == 0, nrecv[0, field, pl.ds(l, 1), :] * inside_s, pltpu.roll(v, 1, 0))
-        high = jnp.where(
-            line == R - 1, nrecv[1, field, pl.ds(l, 1), :] * inside_n, pltpu.roll(v, R - 1, 0)
-        )
-        left = jnp.where(
-            lane == 0, pltpu.roll(erecv[0, field], lax.rem(X - l, X), 1) * inside_w, pltpu.roll(v, 1, 1)
-        )
-        right = jnp.where(
-            lane == X - 1, pltpu.roll(erecv[1, field], X - 1 - l, 1) * inside_e,
-            pltpu.roll(v, X - 1, 1),
-        )
-        return v + diffusion * (low + high + left + right - 4.0 * v)
-
-    def last(l, carry):
-        gain = hk[pl.ds(pl.multiple_of(R * l, R), R), :] + psum * (ds[l] - ds[l + 1])
-        adv_ref[l] = smooth(l, 0, t_ref[l]) + gain * (2.0 / G)
-        hum_ref[l] = smooth(l, 1, q_ref[l])
-        return carry
-
-    lax.fori_loop(0, L, last, 0)
+    halo_ref[0] = erecv[0] * (gx > 0).astype(f32)
+    halo_ref[1] = erecv[1] * (gx < N_GX - 1).astype(f32)
+    halo_ref[2] = nrecv[0] * (gy > 0).astype(f32)
+    halo_ref[3] = nrecv[1] * (gy < N_GY - 1).astype(f32)
     for copy in sends:
         copy.wait()
     srecv[gx] = ssend[gx]
-    slot_ref[...] = srecv[:, 0:CAP, :]
+    slot_ref[...] = srecv[...]
+
+
+def finish(t_ref, q_ref, gain_ref, halo_ref, slot_ref, adv_ref, hum_ref, out_ref):
+    lane = lax.broadcasted_iota(jnp.int32, (R, X), 1)
+    line = lax.broadcasted_iota(jnp.int32, (R, X), 0)
+
+    def smooth(l, field, v):
+        low = jnp.where(line == 0, halo_ref[2, field, l:l + 1, :], pltpu.roll(v, 1, 0))
+        high = jnp.where(line == R - 1, halo_ref[3, field, l:l + 1, :], pltpu.roll(v, R - 1, 0))
+        left = jnp.where(
+            lane == 0, pltpu.roll(halo_ref[0, field], (X - l) % X, 1), pltpu.roll(v, 1, 1)
+        )
+        right = jnp.where(
+            lane == X - 1, pltpu.roll(halo_ref[1, field], X - 1 - l, 1), pltpu.roll(v, X - 1, 1)
+        )
+        return v + diffusion * (low + high + left + right - 4.0 * v)
+
+    for l in range(L):
+        adv_ref[l] = smooth(l, 0, t_ref[l]) + gain_ref[l]
+        hum_ref[l] = smooth(l, 1, q_ref[l])
+    out_ref[...] = slot_ref[:, 0:CAP, :]
 
 
 def on_device(t, q, c, sun, lit, owner, table, cond, planck, insol):
@@ -295,12 +288,16 @@
     field = scratch((L, R, X), f32)
     levels = scratch((L, GP, W2), bf16)
     state = scratch((GP, W2), bf16)
-    out = pl.pallas_call(
+    own = owner[0, :, 0]
+    earlier = jnp.arange(R)[None, :] < jnp.arange(R)[:, None]
+    rank = jnp.sum(jnp.logical_and(own[:, None] == own[None, :], earlier), axis=1)
+    place = (own * 8 + rank).astype(f32)[None]
+    gain, halo, slots = pl.pallas_call(
         kernel,
         out_shape=(
             jax.ShapeDtypeStruct((L, R, X), f32),
-            jax.ShapeDtypeStruct((L, R, X), f32),
-            jax.ShapeDtypeStruct((N_GX, CAP, X), f32),
+            jax.ShapeDtypeStruct((4, 2, R, X), f32),
+            jax.ShapeDtypeStruct((N_GX, 8, X), f32),
         ),
         in_specs=[vmem] * 4 + [pl.BlockSpec(memory_space=pltpu.SMEM)] + [vmem] * 5,
         out_specs=(vmem,) * 3,
@@ -321,8 +318,19 @@
         compiler_params=pltpu.CompilerParams(
             collective_id=0, has_side_effects=True, vmem_limit_bytes=56 * 2**20
         ),
-    )(t, q, c, sun, lit, owner, table, cond[None], planck[None], insol[None])
-    return out[0], out[1], out[2][None, None]
+    )(t, q, c, sun, lit, place, table, cond[None], planck[None], insol[None])
+    adv, hum, filled = pl.pallas_call(
+        finish,
+        out_shape=(
+            jax.ShapeDtypeStruct((L, R, X), f32),
+            jax.ShapeDtypeStruct((L, R, X), f32),
+            jax.ShapeDtypeStruct((N_GX, CAP, X), f32),
+        ),
+        in_specs=[vmem] * 5,
+        out_specs=(vmem,) * 3,
+        compiler_params=pltpu.CompilerParams(vmem_limit_bytes=16 * 2**20),
+    )(t, q, gain, halo, slots)
+    return adv, hum, filled[None, None]
 
 
 def solution(mesh):

time: 57.4 us -> 58.4 us (1.017)
  other arithmetic: 0 us -> 2.08 us
  local copies, waits for them, and re-layouts: 4.64 us -> 2.77 us
  Pallas kernels: 51.9 us -> 52.6 us
    pallas_call x0 -> x1, Pallas kernels: none -> 2 us  [on_device(): pl.pallas_call(finish, out_shape=(jax.ShapeDtypeStruct((L, R, X), f32), j...]
    unnamed x8 -> x10, local copies, waits for them, and re-layouts: 4.64 us -> 2.77 us
    pallas_call x1, Pallas kernels: 51.9 us -> 50.6 us  [on_device(): pl.pallas_call(kernel, out_shape=(jax.ShapeDtypeStruct((L, R, X), f32), j...]
    convert_element_type x0 -> x1, other arithmetic: none -> 1.18 us  [on_device(): place = (own * 8 + rank).astype(f32)[None]]
    reduce_sum x0 -> x1, other arithmetic: none -> 0.91 us  [on_device(): jnp.sum(jnp.logical_and(own[:, None] == own[None, :], earlier), axis=1)]
where the time goes in v3:
time: 58.4 us; the launch traced here: 58.1 us
  Pallas kernels  52.6 us (90%)
  local copies, waits for them, and re-layouts  2.77 us (5%)
  other arithmetic  2.08 us (4%)
  between operations  0.67 us (1%)
    pallas_call x1, Pallas kernels, on_device(): pl.pallas_call(kernel, out_shape=(jax.ShapeDtypeStruct((L, R, X), f32), j...  50.6 us
    unnamed x10, local copies, waits for them, and re-layouts  2.77 us
    pallas_call x1, Pallas kernels, on_device(): pl.pallas_call(finish, out_shape=(jax.ShapeDtypeStruct((L, R, X), f32), j...  2 us
    convert_element_type x1, other arithmetic, on_device(): place = (own * 8 + rank).astype(f32)[None]  1.18 us

profile of v3, /device:TPU:1, one launch (start us, length us, event | category | flops | bytes accessed | tf_op | source)
XLA Modules:
  0.0 58.1 jit_solution(2102347912816407360)
XLA Ops:
  0.6 0.9 %convert_reduce_fusion = s32[32]{0:T(128)S(1)} fusion(s32[32]{0:T(128)} %bitcast.15), kind=kLoop, calls=%fused_computation | loop fusion | flops 5088 | bytes 256 | tf_op jit(solution)/shard_map/reduce_sum | solution.py:293
  1.5 1.2 %fusion.1.place_ref = f32[1,32]{1,0:T(1,128)} fusion(s32[32]{0:T(128)S(1)} %convert_reduce_fusion, s32[1,32,1]{1,2,0:T(1,128)} %param.15), kind=kLoop, calls=%fused_computation.4 | loop fusion | flops 96 | bytes 384 | tf_op jit(solution)/shard_map/convert_element_type | solution.py:294
  2.7 0.0 copy-start
  2.7 0.0 copy-start.1
  2.7 50.6 %shard_map.121 = (f32[30,32,128]{2,1,0:T(8,128)}, f32[4,2,32,128]{3,2,1,0:T(8,128)}, f32[16,8,128]{2,1,0:T(8,128)}) custom-call(f32[30,32,128]{2,1,0:T(8,128)} %t_ref.3, f32[30,32,128]{2,1,0:T(8,128)} %q_ref.3, f32[30,32,128]{2,1,0:T(8,128)} %c_ref.1, f32[32,128]{1,0:T(8,128)} %sun_ref.1, s32[1,32]{1,0:T(1,128)} %lit_ref.1, f32[1,32]{1,0:T(1,128)} %fusion.1.place_ref, ...), custom_call_target="tpu_custom_call" | custom-call | tf_op jit(solution)/shard_map/pallas_call | solution.py:295
  53.3 0.0 copy-done
  53.3 0.0 copy-done.1
  53.4 0.0 copy-start.2
  53.4 1.0 %copy-done.2 = f32[30,32,128]{2,1,0:T(8,128)S(1)} copy-done((f32[30,32,128]{2,1,0:T(8,128)S(1)}, f32[30,32,128]{2,1,0:T(8,128)}, u32[]{:S(2)}) %copy-start.2) | copy-done | bytes 491544
  54.4 0.0 copy-start.3
  54.4 0.9 %copy-done.3 = f32[4,2,32,128]{3,2,1,0:T(8,128)S(1)} copy-done((f32[4,2,32,128]{3,2,1,0:T(8,128)S(1)}, f32[4,2,32,128]{3,2,1,0:T(8,128)}, u32[]{:S(2)}) %copy-start.3) | copy-done | bytes 131096
  55.3 0.0 copy-start.4
  55.3 0.8 %copy-done.4 = f32[16,8,128]{2,1,0:T(8,128)S(1)} copy-done((f32[16,8,128]{2,1,0:T(8,128)S(1)}, f32[16,8,128]{2,1,0:T(8,128)}, u32[]{:S(2)}) %copy-start.4) | copy-done | bytes 65560
  56.1 2.0 %shard_map.122 = (f32[30,32,128]{2,1,0:T(8,128)}, f32[30,32,128]{2,1,0:T(8,128)}, f32[16,4,128]{2,1,0:T(4,128)}) custom-call(f32[30,32,128]{2,1,0:T(8,128)S(1)} %copy-done, f32[30,32,128]{2,1,0:T(8,128)S(1)} %copy-done.1, f32[30,32,128]{2,1,0:T(8,128)S(1)} %copy-done.2, f32[4,2,32,128]{3,2,1,0:T(8,128)S(1)} %copy-done.3, f32[16,8,128]{2,1,0:T(8,128)S(1)} %copy-done.4), custom_call_target="tpu_custom_call" | custom-call | tf_op jit(solution)/shard_map/pallas_call | solution.py:322
Async XLA Ops:
  2.7 50.6 %copy-start = (f32[30,32,128]{2,1,0:T(8,128)S(1)}, f32[30,32,128]{2,1,0:T(8,128)}, u32[]{:S(2)}) copy-start(f32[30,32,128]{2,1,0:T(8,128)} %t_ref.3) | copy-start | bytes 1474564
  2.7 50.6 %copy-start.1 = (f32[30,32,128]{2,1,0:T(8,128)S(1)}, f32[30,32,128]{2,1,0:T(8,128)}, u32[]{:S(2)}) copy-start(f32[30,32,128]{2,1,0:T(8,128)} %q_ref.3) | copy-start | bytes 1474564
  53.4 1.0 %copy-start.2 = (f32[30,32,128]{2,1,0:T(8,128)S(1)}, f32[30,32,128]{2,1,0:T(8,128)}, u32[]{:S(2)}) copy-start(f32[30,32,128]{2,1,0:T(8,128)} %get-tuple-element.9.gain_ref) | copy-start | bytes 1474564
  54.4 0.9 %copy-start.3 = (f32[4,2,32,128]{3,2,1,0:T(8,128)S(1)}, f32[4,2,32,128]{3,2,1,0:T(8,128)}, u32[]{:S(2)}) copy-start(f32[4,2,32,128]{3,2,1,0:T(8,128)} %get-tuple-element.10.halo_ref) | copy-start | bytes 393220
  55.3 0.8 %copy-start.4 = (f32[16,8,128]{2,1,0:T(8,128)S(1)}, f32[16,8,128]{2,1,0:T(8,128)}, u32[]{:S(2)}) copy-start(f32[16,8,128]{2,1,0:T(8,128)} %get-tuple-element.11.slot_ref) | copy-start | bytes 196612

commit v4 on v2

--- a/solution.py
+++ b/solution.py
@@ -12,7 +12,7 @@
 PAIRS = R // 2
 CAP = 4
 N_GX, N_GY = 16, 8
-CH = 5
+CH = 10
 NK = L // CH
 diffusion = 0.2
 diffusivity = 1.66
@@ -84,20 +84,6 @@
         for side in range(2):
             esend[side, field] = edges[2 * field + side]
 
-    pl.semaphore_wait(barrier, N_GX + 1)
-    west, east = {"gx": lax.rem(gx + N_GX - 1, N_GX), "gy": gy}, {"gx": lax.rem(gx + 1, N_GX), "gy": gy}
-    south, north = {"gx": gx, "gy": lax.rem(gy + N_GY - 1, N_GY)}, {"gx": gx, "gy": lax.rem(gy + 1, N_GY)}
-    halos = []
-    for n, (src, dst, target) in enumerate((
-        (esend.at[0], erecv.at[1], west), (esend.at[1], erecv.at[0], east),
-        (nsend.at[0], nrecv.at[1], south), (nsend.at[1], nrecv.at[0], north),
-    )):
-        halos.append(pltpu.make_async_remote_copy(
-            src_ref=src, dst_ref=dst, send_sem=halo_out.at[n], recv_sem=halo_in.at[n],
-            device_id=target, device_id_type=pl.DeviceIdType.MESH,
-        ))
-        halos[-1].start()
-
     i8 = lax.broadcasted_iota(jnp.int32, (NQ, W2), 0).astype(f32)
     ex = (lax.broadcasted_iota(jnp.int32, (16, W2), 0) < 2).astype(f32)
     lr = lax.broadcasted_iota(jnp.int32, (32, 16 * L), 0)
@@ -220,6 +206,20 @@
     chunks(lambda k: next_and_down(0, k, 0))
     down_sums(0)
 
+    pl.semaphore_wait(barrier, N_GX + 1)
+    west, east = {"gx": lax.rem(gx + N_GX - 1, N_GX), "gy": gy}, {"gx": lax.rem(gx + 1, N_GX), "gy": gy}
+    south, north = {"gx": gx, "gy": lax.rem(gy + N_GY - 1, N_GY)}, {"gx": gx, "gy": lax.rem(gy + 1, N_GY)}
+    halos = []
+    for n, (src, dst, target) in enumerate((
+        (esend.at[0], erecv.at[1], west), (esend.at[1], erecv.at[0], east),
+        (nsend.at[0], nrecv.at[1], south), (nsend.at[1], nrecv.at[0], north),
+    )):
+        halos.append(pltpu.make_async_remote_copy(
+            src_ref=src, dst_ref=dst, send_sem=halo_out.at[n], recv_sem=halo_in.at[n],
+            device_id=target, device_id_type=pl.DeviceIdType.MESH,
+        ))
+        halos[-1].start()
+
     def two(i, carry):
         whole(2 * i + 1, 1)
         whole(2 * i + 2, 0)
@@ -229,10 +229,10 @@
     whole(PAIRS - 1, 1)
 
     surface = (sf[...] + psum * ss[L - 1]) * (1.0 / G)
-    own = own_ref[...].reshape(R, 1).astype(f32)
+    own_row = own_ref[...].astype(f32)
     er = lax.broadcasted_iota(jnp.int32, (R, R), 0)
     ec = lax.broadcasted_iota(jnp.int32, (R, R), 1)
-    own_row = jnp.sum(jnp.where(er == ec, own, 0.0), axis=0, keepdims=True)
+    own = jnp.sum(jnp.where(er == ec, own_row, 0.0), axis=1, keepdims=True)
     rank = jnp.sum(
         jnp.where(jnp.logical_and(er < ec, own == own_row), 1.0, 0.0), axis=0, keepdims=True
     )
@@ -321,7 +321,7 @@
         compiler_params=pltpu.CompilerParams(
             collective_id=0, has_side_effects=True, vmem_limit_bytes=56 * 2**20
         ),
-    )(t, q, c, sun, lit, owner, table, cond[None], planck[None], insol[None])
+    )(t, q, c, sun, lit, owner.reshape(1, R), table, cond[None], planck[None], insol[None])
     return out[0], out[1], out[2][None, None]
 
 

time: 57.4 us -> 52.5 us (0.915)
  Pallas kernels: 51.9 us -> 48.4 us
  local copies, waits for them, and re-layouts: 4.64 us -> 3.3 us
    pallas_call x1, Pallas kernels: 51.9 us -> 48.4 us  [on_device(): pl.pallas_call(kernel, out_shape=(jax.ShapeDtypeStruct((L, R, X), f32), j...]
    unnamed x8 -> x7, local copies, waits for them, and re-layouts: 4.64 us -> 3.3 us
where the time goes in v4:
time: 52.5 us; the launch traced here: 52.4 us
  Pallas kernels  48.4 us (92%)
  local copies, waits for them, and re-layouts  3.3 us (6%)
  between operations  0.66 us (1%)
    pallas_call x1, Pallas kernels, on_device(): pl.pallas_call(kernel, out_shape=(jax.ShapeDtypeStruct((L, R, X), f32), j...  48.4 us
    unnamed x7, local copies, waits for them, and re-layouts  3.3 us

profile of v4, /device:TPU:1, one launch (start us, length us, event | category | flops | bytes accessed | tf_op | source)
XLA Modules:
  0.0 52.4 jit_solution(12203989802777506745)
XLA Ops:
  0.6 48.4 %shard_map.121 = (f32[30,32,128]{2,1,0:T(8,128)}, f32[30,32,128]{2,1,0:T(8,128)}, f32[16,4,128]{2,1,0:T(4,128)}) custom-call(f32[30,32,128]{2,1,0:T(8,128)} %t_ref.1, f32[30,32,128]{2,1,0:T(8,128)} %q_ref.1, f32[30,32,128]{2,1,0:T(8,128)} %c_ref.1, f32[32,128]{1,0:T(8,128)} %sun_ref.1, s32[1,32]{1,0:T(1,128)} %lit_ref.1, s32[1,32]{1,0:T(1,128)} %bitcast.9, ...), custom_call_target="tpu_custom_call" | custom-call | tf_op jit(solution)/shard_map/pallas_call | solution.py:298
  49.0 0.0 copy-start
  49.1 0.0 copy-start.1
  49.1 1.9 %copy.16 = f32[30,32,128]{2,1,0:T(8,128)} copy(f32[30,32,128]{2,1,0:T(8,128)} %get-tuple-element.12) | data formatting | bytes 983040
  51.0 0.0 copy-done
  51.0 0.8 %copy.17 = f32[30,32,128]{2,1,0:T(8,128)} copy(f32[30,32,128]{2,1,0:T(8,128)S(1)} %copy-done) | data formatting | bytes 983040
  51.7 0.0 copy-done.1
  51.7 0.6 %copy.18 = f32[1,1,16,4,128]{4,3,2,1,0:T(4,128)} copy(f32[1,1,16,4,128]{4,3,2,1,0:T(4,128)S(1)} %bitcast.5) | data formatting | bytes 65536
Async XLA Ops:
  49.0 1.9 %copy-start = (f32[30,32,128]{2,1,0:T(8,128)S(1)}, f32[30,32,128]{2,1,0:T(8,128)}, u32[]{:S(2)}) copy-start(f32[30,32,128]{2,1,0:T(8,128)} %get-tuple-element.13) | copy-start | bytes 1474564
  49.1 2.7 %copy-start.1 = (f32[16,4,128]{2,1,0:T(4,128)S(1)}, f32[16,4,128]{2,1,0:T(4,128)}, u32[]{:S(2)}) copy-start(f32[16,4,128]{2,1,0:T(4,128)} %get-tuple-element.8) | copy-start | bytes 98308

commit v5 on v4

--- a/solution.py
+++ b/solution.py
@@ -22,7 +22,7 @@
 
 def kernel(
     t_ref, q_ref, c_ref, sun_ref, lit_ref, own_ref, tab_ref, cond_ref, planck_ref, insol_ref,
-    adv_ref, hum_ref, slot_ref,
+    gain_ref, halo_ref, slot_ref,
     hp, cb, ss, ds, th, tabs, pg, qg, tr_a, tr_b, pd_a, pd_b, zacc, bacc, hk, hz, inc, sf,
     xb, Es, Ss, Fs, iv, nsend, nrecv, esend, erecv, ssend, srecv,
     halo_out, halo_in, slot_out, slot_in,
@@ -49,7 +49,6 @@
     chi = ccol.astype(bf16).astype(f32)
     cext = jnp.where(lane16 == 0, chi, jnp.where(lane16 == 1, ccol - chi, 0.0)).astype(bf16)
     lane = lax.broadcasted_iota(jnp.int32, (R, X), 1)
-    line = lax.broadcasted_iota(jnp.int32, (R, X), 0)
     nsend[...] = jnp.zeros_like(nsend)
     ds[0] = jnp.zeros((R, X), f32)
 
@@ -256,38 +255,45 @@
     up_sums(PAIRS - 1)
 
     hk[0:R] = hk[0:R] + qsum * inc[...]
+    for l in range(L):
+        gain_ref[l] = (hk[R * l:R * l + R] + psum * (ds[l] - ds[l + 1])) * (2.0 / G)
     for copy in halos:
         copy.wait()
-    inside_w = (gx > 0).astype(f32)
-    inside_e = (gx < N_GX - 1).astype(f32)
-    inside_s = (gy > 0).astype(f32)
-    inside_n = (gy < N_GY - 1).astype(f32)
-
-    def smooth(l, field, v):
-        low = jnp.where(line == 0, nrecv[0, field, pl.ds(l, 1), :] * inside_s, pltpu.roll(v, 1, 0))
-        high = jnp.where(
-            line == R - 1, nrecv[1, field, pl.ds(l, 1), :] * inside_n, pltpu.roll(v, R - 1, 0)
-        )
-        left = jnp.where(
-            lane == 0, pltpu.roll(erecv[0, field], lax.rem(X - l, X), 1) * inside_w, pltpu.roll(v, 1, 1)
-        )
-        right = jnp.where(
-            lane == X - 1, pltpu.roll(erecv[1, field], X - 1 - l, 1) * inside_e,
-            pltpu.roll(v, X - 1, 1),
-        )
-        return v + diffusion * (low + high + left + right - 4.0 * v)
-
-    def last(l, carry):
-        gain = hk[pl.ds(pl.multiple_of(R * l, R), R), :] + psum * (ds[l] - ds[l + 1])
-        adv_ref[l] = smooth(l, 0, t_ref[l]) + gain * (2.0 / G)
-        hum_ref[l] = smooth(l, 1, q_ref[l])
-        return carry
-
-    lax.fori_loop(0, L, last, 0)
+    halo_ref[0] = erecv[0] * (gx > 0).astype(f32)
+    halo_ref[1] = erecv[1] * (gx < N_GX - 1).astype(f32)
+    halo_ref[2] = nrecv[0] * (gy > 0).astype(f32)
+    halo_ref[3] = nrecv[1] * (gy < N_GY - 1).astype(f32)
     for copy in sends:
         copy.wait()
     srecv[gx] = ssend[gx]
-    slot_ref[...] = srecv[:, 0:CAP, :]
+    slot_ref[...] = srecv[...]
+
+
+LB = 10
+
+
+def finish(t_ref, q_ref, gain_ref, halo_ref, slot_ref, adv_ref, hum_ref, out_ref):
+    lane = lax.broadcasted_iota(jnp.int32, (R, X), 1)
+    line = lax.broadcasted_iota(jnp.int32, (R, X), 0)
+    first = pl.program_id(0) * LB
+
+    def smooth(l, field, v):
+        low = jnp.where(line == 0, halo_ref[2, field, pl.ds(l, 1), :], pltpu.roll(v, 1, 0))
+        high = jnp.where(
+            line == R - 1, halo_ref[3, field, pl.ds(l, 1), :], pltpu.roll(v, R - 1, 0)
+        )
+        left = jnp.where(
+            lane == 0, pltpu.roll(halo_ref[0, field], lax.rem(X - l, X), 1), pltpu.roll(v, 1, 1)
+        )
+        right = jnp.where(
+            lane == X - 1, pltpu.roll(halo_ref[1, field], X - 1 - l, 1), pltpu.roll(v, X - 1, 1)
+        )
+        return v + diffusion * (low + high + left + right - 4.0 * v)
+
+    for j in range(LB):
+        adv_ref[j] = smooth(first + j, 0, t_ref[j]) + gain_ref[j]
+        hum_ref[j] = smooth(first + j, 1, q_ref[j])
+    out_ref[...] = slot_ref[:, 0:CAP, :]
 
 
 def on_device(t, q, c, sun, lit, owner, table, cond, planck, insol):
@@ -295,12 +301,12 @@
     field = scratch((L, R, X), f32)
     levels = scratch((L, GP, W2), bf16)
     state = scratch((GP, W2), bf16)
-    out = pl.pallas_call(
+    gain, halo, slots = pl.pallas_call(
         kernel,
         out_shape=(
             jax.ShapeDtypeStruct((L, R, X), f32),
-            jax.ShapeDtypeStruct((L, R, X), f32),
-            jax.ShapeDtypeStruct((N_GX, CAP, X), f32),
+            jax.ShapeDtypeStruct((4, 2, R, X), f32),
+            jax.ShapeDtypeStruct((N_GX, 8, X), f32),
         ),
         in_specs=[vmem] * 4 + [pl.BlockSpec(memory_space=pltpu.SMEM)] + [vmem] * 5,
         out_specs=(vmem,) * 3,
@@ -322,7 +328,24 @@
             collective_id=0, has_side_effects=True, vmem_limit_bytes=56 * 2**20
         ),
     )(t, q, c, sun, lit, owner.reshape(1, R), table, cond[None], planck[None], insol[None])
-    return out[0], out[1], out[2][None, None]
+    some = pl.BlockSpec((LB, R, X), lambda i: (i, 0, 0))
+    adv, hum, filled = pl.pallas_call(
+        finish,
+        grid=(L // LB,),
+        out_shape=(
+            jax.ShapeDtypeStruct((L, R, X), f32),
+            jax.ShapeDtypeStruct((L, R, X), f32),
+            jax.ShapeDtypeStruct((N_GX, CAP, X), f32),
+        ),
+        in_specs=[
+            some, some, some,
+            pl.BlockSpec((4, 2, R, X), lambda i: (0, 0, 0, 0)),
+            pl.BlockSpec((N_GX, 8, X), lambda i: (0, 0, 0)),
+        ],
+        out_specs=(some, some, pl.BlockSpec((N_GX, CAP, X), lambda i: (0, 0, 0))),
+        compiler_params=pltpu.CompilerParams(vmem_limit_bytes=60 * 2**20),
+    )(t, q, gain, halo, slots)
+    return adv, hum, filled[None, None]
 
 
 def solution(mesh):

time: 52.5 us -> 53.1 us (1.011)
  Pallas kernels: 48.4 us -> 52.2 us
  local copies, waits for them, and re-layouts: 3.3 us -> 0 us
    pallas_call x0 -> x1, Pallas kernels: none -> 3.96 us  [on_device(): pl.pallas_call(finish, grid=(L // LB,), out_shape=(jax.ShapeDtypeStruct((...]
    unnamed x7 -> x0, local copies, waits for them, and re-layouts: 3.3 us -> none
where the time goes in v5:
time: 53.1 us; the launch traced here: 52.9 us
  Pallas kernels  52.2 us (98%)
  between operations  0.64 us (1%)
    pallas_call x1, Pallas kernels, on_device(): pl.pallas_call(kernel, out_shape=(jax.ShapeDtypeStruct((L, R, X), f32), j...  48.3 us
    pallas_call x1, Pallas kernels, on_device(): pl.pallas_call(finish, grid=(L // LB,), out_shape=(jax.ShapeDtypeStruct((...  3.96 us

profile of v5, /device:TPU:1, one launch (start us, length us, event | category | flops | bytes accessed | tf_op | source)
XLA Modules:
  0.0 52.9 jit_solution(8441837138086788014)
XLA Ops:
  0.6 48.3 %shard_map.121 = (f32[30,32,128]{2,1,0:T(8,128)}, f32[4,2,32,128]{3,2,1,0:T(8,128)}, f32[16,8,128]{2,1,0:T(8,128)}) custom-call(f32[30,32,128]{2,1,0:T(8,128)} %t_ref.3, f32[30,32,128]{2,1,0:T(8,128)} %q_ref.3, f32[30,32,128]{2,1,0:T(8,128)} %c_ref.1, f32[32,128]{1,0:T(8,128)} %sun_ref.1, s32[1,32]{1,0:T(1,128)} %lit_ref.1, s32[1,32]{1,0:T(1,128)} %bitcast.8, ...), custom_call_target="tpu_custom_call" | custom-call | tf_op jit(solution)/shard_map/pallas_call | solution.py:304
  48.9 4.0 %shard_map.122 = (f32[30,32,128]{2,1,0:T(8,128)}, f32[30,32,128]{2,1,0:T(8,128)}, f32[16,4,128]{2,1,0:T(4,128)}) custom-call(f32[30,32,128]{2,1,0:T(8,128)} %t_ref.3, f32[30,32,128]{2,1,0:T(8,128)} %q_ref.3, f32[30,32,128]{2,1,0:T(8,128)} %get-tuple-element.9.gain_ref, f32[4,2,32,128]{3,2,1,0:T(8,128)} %get-tuple-element.10.halo_ref, ...), custom_call_target="tpu_custom_call" | custom-call | tf_op jit(solution)/shard_map/pallas_call | solution.py:332

commit v6 on v4

--- a/solution.py
+++ b/solution.py
@@ -53,6 +53,8 @@
     nsend[...] = jnp.zeros_like(nsend)
     ds[0] = jnp.zeros((R, X), f32)
 
+    none = jnp.zeros((R, X), f32)
+
     def prepare(l, edges):
         tabs[l, :, 0:NT * NQ] = jnp.concatenate(
             [tab_ref[l].astype(f32) * SCALE, jnp.zeros((GP - G, NT * NQ), f32)], axis=0
@@ -61,8 +63,13 @@
         warm, wet = t_ref[l], q_ref[l]
         t = warm.astype(bf16).astype(f32)
         tp = jnp.clip((t + 3.0) * ((NT - 1.0) / 6.0), 0.0, NT - 1.0)
+        node = jnp.floor(tp)
+        f = tp - node
+        below, above = 1.0 - f, none
         for i in range(NT):
-            th[l, i] = jnp.maximum(0.0, 1.0 - jnp.abs(tp - float(i)))
+            at = node == float(i)
+            th[l, i] = jnp.where(at, below, above)
+            above = jnp.where(at, f, none)
         s = 1.0 + 0.25 * t
         ss[l] = s
         ds[l] = edges[4] - s
@@ -77,7 +84,6 @@
             out.append(jnp.where(here, pltpu.roll(v, l + 1, 1), edges[2 * field + 1]))
         return tuple(out) + (s,)
 
-    none = jnp.zeros((R, X), f32)
     edges = lax.fori_loop(0, L, prepare, (none,) * 5)
     ds[L] = none
     for field in range(2):
@@ -277,13 +283,15 @@
         )
         return v + diffusion * (low + high + left + right - 4.0 * v)
 
-    def last(l, carry):
-        gain = hk[pl.ds(pl.multiple_of(R * l, R), R), :] + psum * (ds[l] - ds[l + 1])
-        adv_ref[l] = smooth(l, 0, t_ref[l]) + gain * (2.0 / G)
-        hum_ref[l] = smooth(l, 1, q_ref[l])
+    def last(i, carry):
+        for j in range(5):
+            l = 5 * i + j
+            gain = hk[pl.ds(pl.multiple_of(R * l, R), R), :] + psum * (ds[l] - ds[l + 1])
+            adv_ref[l] = smooth(l, 0, t_ref[l]) + gain * (2.0 / G)
+            hum_ref[l] = smooth(l, 1, q_ref[l])
         return carry
 
-    lax.fori_loop(0, L, last, 0)
+    lax.fori_loop(0, L // 5, last, 0)
     for copy in sends:
         copy.wait()
     srecv[gx] = ssend[gx]

time: 52.5 us -> 52.5 us (level)
  no operation moved by 1% of the time
where the time goes in v6:
time: 52.5 us; the launch traced here: 52.4 us
  Pallas kernels  48.4 us (92%)
  local copies, waits for them, and re-layouts  3.3 us (6%)
  between operations  0.66 us (1%)
    pallas_call x1, Pallas kernels, on_device(): pl.pallas_call(kernel, out_shape=(jax.ShapeDtypeStruct((L, R, X), f32), j...  48.4 us
    unnamed x7, local copies, waits for them, and re-layouts  3.3 us

profile of v6, /device:TPU:1, one launch (start us, length us, event | category | flops | bytes accessed | tf_op | source)
XLA Modules:
  0.0 52.4 jit_solution(18279596266429131964)
XLA Ops:
  0.6 48.4 %shard_map.121 = (f32[30,32,128]{2,1,0:T(8,128)}, f32[30,32,128]{2,1,0:T(8,128)}, f32[16,4,128]{2,1,0:T(4,128)}) custom-call(f32[30,32,128]{2,1,0:T(8,128)} %t_ref.1, f32[30,32,128]{2,1,0:T(8,128)} %q_ref.1, f32[30,32,128]{2,1,0:T(8,128)} %c_ref.1, f32[32,128]{1,0:T(8,128)} %sun_ref.1, s32[1,32]{1,0:T(1,128)} %lit_ref.1, s32[1,32]{1,0:T(1,128)} %bitcast.9, ...), custom_call_target="tpu_custom_call" | custom-call | tf_op jit(solution)/shard_map/pallas_call | solution.py:306
  49.0 0.0 copy-start
  49.1 0.0 copy-start.1
  49.1 1.9 %copy.16 = f32[30,32,128]{2,1,0:T(8,128)} copy(f32[30,32,128]{2,1,0:T(8,128)} %get-tuple-element.12) | data formatting | bytes 983040
  51.0 0.0 copy-done
  51.0 0.8 %copy.17 = f32[30,32,128]{2,1,0:T(8,128)} copy(f32[30,32,128]{2,1,0:T(8,128)S(1)} %copy-done) | data formatting | bytes 983040
  51.7 0.0 copy-done.1
  51.7 0.6 %copy.18 = f32[1,1,16,4,128]{4,3,2,1,0:T(4,128)} copy(f32[1,1,16,4,128]{4,3,2,1,0:T(4,128)S(1)} %bitcast.5) | data formatting | bytes 65536
Async XLA Ops:
  49.0 1.9 %copy-start = (f32[30,32,128]{2,1,0:T(8,128)S(1)}, f32[30,32,128]{2,1,0:T(8,128)}, u32[]{:S(2)}) copy-start(f32[30,32,128]{2,1,0:T(8,128)} %get-tuple-element.13) | copy-start | bytes 1474564
  49.1 2.7 %copy-start.1 = (f32[16,4,128]{2,1,0:T(4,128)S(1)}, f32[16,4,128]{2,1,0:T(4,128)}, u32[]{:S(2)}) copy-start(f32[16,4,128]{2,1,0:T(4,128)} %get-tuple-element.8) | copy-start | bytes 98308

commit v7 on v6

--- a/solution.py
+++ b/solution.py
@@ -296,6 +296,19 @@
         copy.wait()
     srecv[gx] = ssend[gx]
     slot_ref[...] = srecv[:, 0:CAP, :]
+
+
+def hand_over(adv_in, hum_in, slot_in, adv_ref, hum_ref, slot_ref, sems):
+    step = L // 3
+    copies = [pltpu.make_async_copy(slot_in, slot_ref, sems.at[6])]
+    for n in range(3):
+        at = pl.ds(n * step, step)
+        copies.append(pltpu.make_async_copy(adv_in.at[at], adv_ref.at[at], sems.at[2 * n]))
+        copies.append(pltpu.make_async_copy(hum_in.at[at], hum_ref.at[at], sems.at[2 * n + 1]))
+    for copy in copies:
+        copy.start()
+    for copy in copies:
+        copy.wait()
 
 
 def on_device(t, q, c, sun, lit, owner, table, cond, planck, insol):
@@ -330,6 +343,15 @@
             collective_id=0, has_side_effects=True, vmem_limit_bytes=56 * 2**20
         ),
     )(t, q, c, sun, lit, owner.reshape(1, R), table, cond[None], planck[None], insol[None])
+    anywhere = pl.BlockSpec(memory_space=pl.ANY)
+    out = pl.pallas_call(
+        hand_over,
+        out_shape=tuple(jax.ShapeDtypeStruct(v.shape, f32) for v in out),
+        in_specs=[anywhere] * 3,
+        out_specs=(anywhere,) * 3,
+        scratch_shapes=[pltpu.SemaphoreType.DMA((7,))],
+        compiler_params=pltpu.CompilerParams(vmem_limit_bytes=60 * 2**20),
+    )(*out)
     return out[0], out[1], out[2][None, None]
 
 

time: 52.5 us -> 81.1 us (1.54)
  Pallas kernels: 48.4 us -> 80.4 us
  local copies, waits for them, and re-layouts: 3.3 us -> 0 us
    pallas_call x0 -> x1, Pallas kernels: none -> 31.9 us  [on_device(): pl.pallas_call(hand_over, out_shape=tuple((jax.ShapeDtypeStruct(v.shape,...]
    unnamed x7 -> x0, local copies, waits for them, and re-layouts: 3.3 us -> none
where the time goes in v7:
time: 81.1 us; the launch traced here: 81 us
  Pallas kernels  80.4 us (99%)
    pallas_call x1, Pallas kernels, on_device(): pl.pallas_call(kernel, out_shape=(jax.ShapeDtypeStruct((L, R, X), f32), j...  48.4 us
    pallas_call x1, Pallas kernels, on_device(): pl.pallas_call(hand_over, out_shape=tuple((jax.ShapeDtypeStruct(v.shape,...  31.9 us

profile of v7, /device:TPU:1, one launch (start us, length us, event | category | flops | bytes accessed | tf_op | source)
XLA Modules:
  0.0 81.0 jit_solution(11360533753249861927)
XLA Ops:
  0.6 48.4 %shard_map.121 = (f32[30,32,128]{2,1,0:T(8,128)}, f32[30,32,128]{2,1,0:T(8,128)}, f32[16,4,128]{2,1,0:T(4,128)}) custom-call(f32[30,32,128]{2,1,0:T(8,128)} %t_ref.1, f32[30,32,128]{2,1,0:T(8,128)} %q_ref.1, f32[30,32,128]{2,1,0:T(8,128)} %c_ref.1, f32[32,128]{1,0:T(8,128)} %sun_ref.1, s32[1,32]{1,0:T(1,128)} %lit_ref.1, s32[1,32]{1,0:T(1,128)} %bitcast.8, ...), custom_call_target="tpu_custom_call" | custom-call | tf_op jit(solution)/shard_map/pallas_call | solution.py:319
  49.1 31.9 %shard_map.122 = (f32[30,32,128]{2,1,0:T(8,128)}, f32[30,32,128]{2,1,0:T(8,128)}, f32[16,4,128]{2,1,0:T(4,128)}) custom-call(f32[30,32,128]{2,1,0:T(8,128)} %get-tuple-element.9.adv_in, f32[30,32,128]{2,1,0:T(8,128)} %get-tuple-element.10.hum_in, f32[16,4,128]{2,1,0:T(4,128)} %get-tuple-element.11.slot_in), custom_call_target="tpu_custom_call" | custom-call | tf_op jit(solution)/shard_map/pallas_call | solution.py:347

commit v8 on v7

--- a/solution.py
+++ b/solution.py
@@ -298,16 +298,21 @@
     slot_ref[...] = srecv[:, 0:CAP, :]
 
 
-def hand_over(adv_in, hum_in, slot_in, adv_ref, hum_ref, slot_ref, sems):
+def hand_over(adv_in, hum_in, slot_in, adv_ref, hum_ref, slot_ref, adv_at, hum_at, slot_at, arrive, leave):
     step = L // 3
-    copies = [pltpu.make_async_copy(slot_in, slot_ref, sems.at[6])]
+    parts = [(slot_in, slot_at, slot_ref)]
     for n in range(3):
         at = pl.ds(n * step, step)
-        copies.append(pltpu.make_async_copy(adv_in.at[at], adv_ref.at[at], sems.at[2 * n]))
-        copies.append(pltpu.make_async_copy(hum_in.at[at], hum_ref.at[at], sems.at[2 * n + 1]))
-    for copy in copies:
+        parts.append((adv_in.at[at], adv_at.at[at], adv_ref.at[at]))
+        parts.append((hum_in.at[at], hum_at.at[at], hum_ref.at[at]))
+    coming = [pltpu.make_async_copy(a, b, arrive.at[n]) for n, (a, b, _) in enumerate(parts)]
+    going = [pltpu.make_async_copy(b, c, leave.at[n]) for n, (_, b, c) in enumerate(parts)]
+    for copy in coming:
         copy.start()
-    for copy in copies:
+    for one, two in zip(coming, going):
+        one.wait()
+        two.start()
+    for copy in going:
         copy.wait()
 
 
@@ -349,7 +354,10 @@
         out_shape=tuple(jax.ShapeDtypeStruct(v.shape, f32) for v in out),
         in_specs=[anywhere] * 3,
         out_specs=(anywhere,) * 3,
-        scratch_shapes=[pltpu.SemaphoreType.DMA((7,))],
+        scratch_shapes=[
+            field, field, scratch((N_GX, CAP, X), f32),
+            pltpu.SemaphoreType.DMA((7,)), pltpu.SemaphoreType.DMA((7,)),
+        ],
         compiler_params=pltpu.CompilerParams(vmem_limit_bytes=60 * 2**20),
     )(*out)
     return out[0], out[1], out[2][None, None]

time: 81.1 us -> 51.3 us (0.63)
  Pallas kernels: 80.4 us -> 50.5 us
    pallas_call x1, Pallas kernels: 31.9 us -> 2.07 us  [on_device(): pl.pallas_call(hand_over, out_shape=tuple((jax.ShapeDtypeStruct(v.shape,...]
where the time goes in v8:
time: 51.3 us; the launch traced here: 51.1 us
  Pallas kernels  50.5 us (98%)
  between operations  0.64 us (1%)
    pallas_call x1, Pallas kernels, on_device(): pl.pallas_call(kernel, out_shape=(jax.ShapeDtypeStruct((L, R, X), f32), j...  48.4 us
    pallas_call x1, Pallas kernels, on_device(): pl.pallas_call(hand_over, out_shape=tuple((jax.ShapeDtypeStruct(v.shape,...  2.07 us

profile of v8, /device:TPU:1, one launch (start us, length us, event | category | flops | bytes accessed | tf_op | source)
XLA Modules:
  0.0 51.1 jit_solution(15772284725653837787)
XLA Ops:
  0.6 48.4 %shard_map.121 = (f32[30,32,128]{2,1,0:T(8,128)}, f32[30,32,128]{2,1,0:T(8,128)}, f32[16,4,128]{2,1,0:T(4,128)}) custom-call(f32[30,32,128]{2,1,0:T(8,128)} %t_ref.1, f32[30,32,128]{2,1,0:T(8,128)} %q_ref.1, f32[30,32,128]{2,1,0:T(8,128)} %c_ref.1, f32[32,128]{1,0:T(8,128)} %sun_ref.1, s32[1,32]{1,0:T(1,128)} %lit_ref.1, s32[1,32]{1,0:T(1,128)} %bitcast.8, ...), custom_call_target="tpu_custom_call" | custom-call | tf_op jit(solution)/shard_map/pallas_call | solution.py:324
  49.1 2.1 %shard_map.122 = (f32[30,32,128]{2,1,0:T(8,128)}, f32[30,32,128]{2,1,0:T(8,128)}, f32[16,4,128]{2,1,0:T(4,128)}) custom-call(f32[30,32,128]{2,1,0:T(8,128)} %get-tuple-element.9.adv_in, f32[30,32,128]{2,1,0:T(8,128)} %get-tuple-element.10.hum_in, f32[16,4,128]{2,1,0:T(4,128)} %get-tuple-element.11.slot_in), custom_call_target="tpu_custom_call" | custom-call | tf_op jit(solution)/shard_map/pallas_call | solution.py:352
